TPU v7x, 512 devices: a whole 4x8x8 slice. The times are simulated.
512 devices in a mesh: leaf: 512 (over z, y, x, core).
Axes of the slice: x: 4, y: 8, z: 8, core: 2. Of those that a mesh axis runs over, the one named last changes fastest.
Arguments:
- right_side_block: bfloat16 [262144, 128], P('leaf'), may hold values from -6 to 6
- leaf_rows: bfloat16 [262144, 4096], P('leaf'), as said below
- bases: bfloat16 [6, 262144, 128], P(None, 'leaf'), as said below
Outputs:
- product: float32 [262144, 128], P('leaf')
Inputs may be any that keep to these rules, and one draw needn't show every extreme that they name: `leaf_rows`: within each leaf the diagonal block is symmetric: row a, column b of leaf n equals row b, column a of leaf n. `bases`: rows of independent entries; each level has its own scale.
All inputs are finite; a program needn't handle non-finite values.
Results may differ from a plain program's by a relative error of at most 0.0025.
Values may be sent and summed in bfloat16 or wider, within the bound.
No kernel may reach another device: no remote copies, remote signals or barrier semaphores. Data moves between devices by JAX's collectives and lax.ppermute only.
A program may use at most 64 MiB of HBM per device.

v0:
```python
import jax
import jax.numpy as jnp
from jax import lax
from jax.sharding import PartitionSpec as P

LEAF_DEVS = 8


def partner(array, axis, distance):
    return lax.ppermute(array, axis, [(i, i ^ 1 << distance) for i in range(lax.axis_size(axis))])


def shards(right_side_block, leaf_rows, bases):
    level_count = bases.shape[0]
    leaf_bits = LEAF_DEVS.bit_length() - 1
    position = lax.axis_index("leaf")
    gathered = right_side_block
    for step_bit in range(leaf_bits):
        received = partner(gathered, "leaf", step_bit)
        high_half = position >> step_bit & 1 == 1
        gathered = jnp.where(
            high_half,
            jnp.concatenate([received, gathered], 0),
            jnp.concatenate([gathered, received], 0),
        )
    diagonal_part = jnp.dot(leaf_rows, gathered, preferred_element_type=jnp.float32)
    partial_totals = jnp.einsum(
        "qip,iw->qpw", bases, right_side_block, preferred_element_type=jnp.float32
    )
    siblings = []
    for depth in range(level_count):
        running_total = partial_totals[depth]
        for step_bit in range(leaf_bits + depth):
            running_total = running_total + partner(running_total, "leaf", step_bit)
        siblings.append(
            partner(running_total.astype(jnp.bfloat16), "leaf", leaf_bits + depth).astype(
                running_total.dtype
            )
        )
    coupling_weights = jnp.stack(siblings, 0).astype(jnp.bfloat16)
    coupled_product = jnp.einsum(
        "txv,tvu->xu", bases, coupling_weights, preferred_element_type=jnp.float32
    )
    return diagonal_part + coupled_product


def solution(mesh):
    in_specs = (P("leaf", None), P("leaf", None), P(None, "leaf", None))
    out_specs = P("leaf", None)
    return jax.shard_map(shards, mesh=mesh, in_specs=in_specs, out_specs=out_specs, check_vma=False)
```

profile of v0, /device:TPU:2, one launch (start us, length us, event | category | flops | bytes accessed | tf_op | source)
XLA Modules:
  0.0 168.4 jit_solution(580055376571105443)
XLA Ops:
  4.4 2.4 %collective-permute-start.18 = (f32[128,128]{1,0:T(8,128)S(1)}, f32[128,128]{1,0:T(8,128)S(1)}, u32[]{:S(2)}, u32[]{:S(2)}) collective-permute-start(f32[128,128]{1,0:T(8,128)S(1)} %get-tuple-element.13), channel_id=1, source_target_pairs={{0,1},{1,0},{2,3},{3,2},{4,5},{5,4},{6,7},{7,6},{8,9},{9,8},{10,11... | collective-permute-start | bytes 196616 | tf_op jit(solution)/shard_map/ppermute | solution.py:10
  16.4 7.8 %collective-permute-start.4 = (f32[128,128]{1,0:T(8,128)S(1)}, f32[128,128]{1,0:T(8,128)S(1)}, u32[]{:S(2)}, u32[]{:S(2)}) collective-permute-start(f32[128,128]{1,0:T(8,128)S(1)} %get-tuple-element.10), channel_id=1, source_target_pairs={{0,2},{1,3},{2,0},{3,1},{4,6},{5,7},{6,4},{7,5},{8,10},{9,11},{10,... | collective-permute-start | bytes 196616 | tf_op jit(solution)/shard_map/ppermute | solution.py:10
  26.2 3.9 %collective-permute-start.26 = (f32[128,128]{1,0:T(8,128)S(1)}, f32[128,128]{1,0:T(8,128)S(1)}, u32[]{:S(2)}, u32[]{:S(2)}) collective-permute-start(f32[128,128]{1,0:T(8,128)S(1)} %get-tuple-element.6), channel_id=1, source_target_pairs={{0,2},{1,3},{2,0},{3,1},{4,6},{5,7},{6,4},{7,5},{8,10},{9,11},{10,... | collective-permute-start | bytes 196616 | tf_op jit(solution)/shard_map/ppermute | solution.py:10
  32.1 3.9 %collective-permute-start.13 = (f32[128,128]{1,0:T(8,128)S(1)}, f32[128,128]{1,0:T(8,128)S(1)}, u32[]{:S(2)}, u32[]{:S(2)}) collective-permute-start(f32[128,128]{1,0:T(8,128)S(1)} %get-tuple-element.8), channel_id=1, source_target_pairs={{0,2},{1,3},{2,0},{3,1},{4,6},{5,7},{6,4},{7,5},{8,10},{9,11},{10,... | collective-permute-start | bytes 196616 | tf_op jit(solution)/shard_map/ppermute | solution.py:10
  41.9 5.4 %collective-permute-start.35 = (f32[128,128]{1,0:T(8,128)S(1)}, f32[128,128]{1,0:T(8,128)S(1)}, u32[]{:S(2)}, u32[]{:S(2)}) collective-permute-start(f32[128,128]{1,0:T(8,128)S(1)} %add.131), channel_id=1, source_target_pairs={{0,4},{1,5},{2,6},{3,7},{4,0},{5,1},{6,2},{7,3},{8,12},{9,13},{10,... | collective-permute-start | bytes 196616 | tf_op jit(solution)/shard_map/ppermute | solution.py:10
  49.3 5.4 %collective-permute-start.20 = (f32[128,128]{1,0:T(8,128)S(1)}, f32[128,128]{1,0:T(8,128)S(1)}, u32[]{:S(2)}, u32[]{:S(2)}) collective-permute-start(f32[128,128]{1,0:T(8,128)S(1)} %add.118), channel_id=1, source_target_pairs={{0,4},{1,5},{2,6},{3,7},{4,0},{5,1},{6,2},{7,3},{8,12},{9,13},{10,... | collective-permute-start | bytes 196616 | tf_op jit(solution)/shard_map/ppermute | solution.py:10
  56.7 5.4 %collective-permute-start.9 = (f32[128,128]{1,0:T(8,128)S(1)}, f32[128,128]{1,0:T(8,128)S(1)}, u32[]{:S(2)}, u32[]{:S(2)}) collective-permute-start(f32[128,128]{1,0:T(8,128)S(1)} %add.109), channel_id=1, source_target_pairs={{0,4},{1,5},{2,6},{3,7},{4,0},{5,1},{6,2},{7,3},{8,12},{9,13},{10,... | collective-permute-start | bytes 196616 | tf_op jit(solution)/shard_map/ppermute | solution.py:10
  64.2 3.9 %collective-permute-start.36 = (f32[128,128]{1,0:T(8,128)S(1)}, f32[128,128]{1,0:T(8,128)S(1)}, u32[]{:S(2)}, u32[]{:S(2)}) collective-permute-start(f32[128,128]{1,0:T(8,128)S(1)} %add.132), channel_id=1, source_target_pairs={{0,8},{1,9},{2,10},{3,11},{4,12},{5,13},{6,14},{7,15},{8,0},{9,1},... | collective-permute-start | bytes 196616 | tf_op jit(solution)/shard_map/ppermute | solution.py:10
  70.1 3.9 %collective-permute-start.21 = (f32[128,128]{1,0:T(8,128)S(1)}, f32[128,128]{1,0:T(8,128)S(1)}, u32[]{:S(2)}, u32[]{:S(2)}) collective-permute-start(f32[128,128]{1,0:T(8,128)S(1)} %add.119), channel_id=1, source_target_pairs={{0,8},{1,9},{2,10},{3,11},{4,12},{5,13},{6,14},{7,15},{8,0},{9,1},... | collective-permute-start | bytes 196616 | tf_op jit(solution)/shard_map/ppermute | solution.py:10
  76.0 3.9 %collective-permute-start.10 = (f32[128,128]{1,0:T(8,128)S(1)}, f32[128,128]{1,0:T(8,128)S(1)}, u32[]{:S(2)}, u32[]{:S(2)}) collective-permute-start(f32[128,128]{1,0:T(8,128)S(1)} %add.110), channel_id=1, source_target_pairs={{0,8},{1,9},{2,10},{3,11},{4,12},{5,13},{6,14},{7,15},{8,0},{9,1},... | collective-permute-start | bytes 196616 | tf_op jit(solution)/shard_map/ppermute | solution.py:10
  80.0 3.9 %collective-permute-start.1 = (bf16[1024,128]{1,0:T(8,128)(2,1)S(1)}, bf16[1024,128]{1,0:T(8,128)(2,1)S(1)}, u32[]{:S(2)}, u32[]{:S(2)}) collective-permute-start(bf16[1024,128]{1,0:T(8,128)(2,1)S(1)} %maximum_select_fusion.3), channel_id=1, source_target_pairs={{0,2},{1,3},{2,0},{3,1},{4,6},{5,7},{6,4},{7,5},{8,10},{9,11},{10,... | collective-permute-start | bytes 786440 | tf_op jit(solution)/shard_map/ppermute | solution.py:10
  85.9 4.8 %collective-permute-start.29 = (f32[128,128]{1,0:T(8,128)S(1)}, f32[128,128]{1,0:T(8,128)S(1)}, u32[]{:S(2)}, u32[]{:S(2)}) collective-permute-start(f32[128,128]{1,0:T(8,128)S(1)} %add.126), channel_id=1, source_target_pairs={{0,16},{1,17},{2,18},{3,19},{4,20},{5,21},{6,22},{7,23},{8,24},{9,... | collective-permute-start | bytes 196616 | tf_op jit(solution)/shard_map/ppermute | solution.py:10
  92.7 4.8 %collective-permute-start.16 = (f32[128,128]{1,0:T(8,128)S(1)}, f32[128,128]{1,0:T(8,128)S(1)}, u32[]{:S(2)}, u32[]{:S(2)}) collective-permute-start(f32[128,128]{1,0:T(8,128)S(1)} %add.115), channel_id=1, source_target_pairs={{0,16},{1,17},{2,18},{3,19},{4,20},{5,21},{6,22},{7,23},{8,24},{9,... | collective-permute-start | bytes 196616 | tf_op jit(solution)/shard_map/ppermute | solution.py:10
  99.9 4.7 %collective-permute-start.11 = (bf16[128,128]{1,0:T(8,128)(2,1)S(1)}, bf16[128,128]{1,0:T(8,128)(2,1)S(1)}, u32[]{:S(2)}, u32[]{:S(2)}) collective-permute-start(bf16[128,128]{1,0:T(8,128)(2,1)S(1)} %add_convert_fusion.4), channel_id=1, source_target_pairs={{0,16},{1,17},{2,18},{3,19},{4,20},{5,21},{6,22},{7,23},{8,24},{9,... | collective-permute-start | bytes 98312 | tf_op jit(solution)/shard_map/ppermute | solution.py:10
  106.6 3.7 %collective-permute-start.17 = (bf16[128,128]{1,0:T(8,128)(2,1)S(1)}, bf16[128,128]{1,0:T(8,128)(2,1)S(1)}, u32[]{:S(2)}, u32[]{:S(2)}) collective-permute-start(bf16[128,128]{1,0:T(8,128)(2,1)S(1)} %add_convert_fusion.3), channel_id=1, source_target_pairs={{0,32},{1,33},{2,34},{3,35},{4,36},{5,37},{6,38},{7,39},{8,40},{9,... | collective-permute-start | bytes 98312 | tf_op jit(solution)/shard_map/ppermute | solution.py:10
  110.4 6.3 %collective-permute-start.38 = (f32[128,128]{1,0:T(8,128)S(1)}, f32[128,128]{1,0:T(8,128)S(1)}, u32[]{:S(2)}, u32[]{:S(2)}) collective-permute-start(f32[128,128]{1,0:T(8,128)S(1)} %add.134), channel_id=1, source_target_pairs={{0,32},{1,33},{2,34},{3,35},{4,36},{5,37},{6,38},{7,39},{8,40},{9,... | collective-permute-start | bytes 196616 | tf_op jit(solution)/shard_map/ppermute | solution.py:10
  116.7 3.7 %collective-permute-start.30 = (f32[128,128]{1,0:T(8,128)S(1)}, f32[128,128]{1,0:T(8,128)S(1)}, u32[]{:S(2)}, u32[]{:S(2)}) collective-permute-start(f32[128,128]{1,0:T(8,128)S(1)} %add.127), channel_id=1, source_target_pairs={{0,32},{1,33},{2,34},{3,35},{4,36},{5,37},{6,38},{7,39},{8,40},{9,... | collective-permute-start | bytes 196616 | tf_op jit(solution)/shard_map/ppermute | solution.py:10
  120.5 6.0 %collective-permute-start.23 = (f32[128,128]{1,0:T(8,128)S(1)}, f32[128,128]{1,0:T(8,128)S(1)}, u32[]{:S(2)}, u32[]{:S(2)}) collective-permute-start(f32[128,128]{1,0:T(8,128)S(1)} %add.121), channel_id=1, source_target_pairs={{0,32},{1,33},{2,34},{3,35},{4,36},{5,37},{6,38},{7,39},{8,40},{9,... | collective-permute-start | bytes 196616 | tf_op jit(solution)/shard_map/ppermute | solution.py:10
  126.6 4.0 %collective-permute-done.23 = f32[128,128]{1,0:T(8,128)S(1)} collective-permute-done((f32[128,128]{1,0:T(8,128)S(1)}, f32[128,128]{1,0:T(8,128)S(1)}, u32[]{:S(2)}, u32[]{:S(2)}) %collective-permute-start.23) | collective-permute-done | bytes 65568 | tf_op jit(solution)/shard_map/ppermute | solution.py:10
  130.6 4.3 %collective-permute-start.24 = (bf16[128,128]{1,0:T(8,128)(2,1)S(1)}, bf16[128,128]{1,0:T(8,128)(2,1)S(1)}, u32[]{:S(2)}, u32[]{:S(2)}) collective-permute-start(bf16[128,128]{1,0:T(8,128)(2,1)S(1)} %add_convert_fusion.2), channel_id=1, source_target_pairs={{0,64},{1,65},{2,66},{3,67},{4,68},{5,69},{6,70},{7,71},{8,72},{9,... | collective-permute-start | bytes 98312 | tf_op jit(solution)/shard_map/ppermute | solution.py:10
  135.0 4.3 %collective-permute-start.2 = (bf16[2048,128]{1,0:T(8,128)(2,1)S(1)}, bf16[2048,128]{1,0:T(8,128)(2,1)S(1)}, u32[]{:S(2)}, u32[]{:S(2)}) collective-permute-start(bf16[2048,128]{1,0:T(8,128)(2,1)S(1)} %maximum_select_fusion.2), channel_id=1, source_target_pairs={{0,4},{1,5},{2,6},{3,7},{4,0},{5,1},{6,2},{7,3},{8,12},{9,13},{10,... | collective-permute-start | bytes 1572872 | tf_op jit(solution)/shard_map/ppermute | solution.py:10
  141.3 3.9 %collective-permute-start.31 = (f32[128,128]{1,0:T(8,128)S(1)}, f32[128,128]{1,0:T(8,128)S(1)}, u32[]{:S(2)}, u32[]{:S(2)}) collective-permute-start(f32[128,128]{1,0:T(8,128)S(1)} %add.128), channel_id=1, source_target_pairs={{0,64},{1,65},{2,66},{3,67},{4,68},{5,69},{6,70},{7,71},{8,72},{9,... | collective-permute-start | bytes 196616 | tf_op jit(solution)/shard_map/ppermute | solution.py:10
  146.2 5.8 %collective-permute-start.40 = (f32[128,128]{1,0:T(8,128)S(1)}, f32[128,128]{1,0:T(8,128)S(1)}, u32[]{:S(2)}, u32[]{:S(2)}) collective-permute-start(f32[128,128]{1,0:T(8,128)S(1)} %add.136), channel_id=1, source_target_pairs={{0,128},{1,129},{2,130},{3,131},{4,132},{5,133},{6,134},{7,135},{8... | collective-permute-start | bytes 196616 | tf_op jit(solution)/shard_map/ppermute | solution.py:10
  154.2 9.4 %collective-permute-start.41 = (bf16[128,128]{1,0:T(8,128)(2,1)S(1)}, bf16[128,128]{1,0:T(8,128)(2,1)S(1)}, u32[]{:S(2)}, u32[]{:S(2)}) collective-permute-start(bf16[128,128]{1,0:T(8,128)(2,1)S(1)} %add_convert_fusion), channel_id=1, source_target_pairs={{0,256},{1,257},{2,258},{3,259},{4,260},{5,261},{6,262},{7,263},{8... | collective-permute-start | bytes 98312 | tf_op jit(solution)/shard_map/ppermute | solution.py:10
  (107 shorter events, 51.7 us)
Async XLA Ops:
  16.4 19.5 %collective-permute-start.4 = (f32[128,128]{1,0:T(8,128)S(1)}, f32[128,128]{1,0:T(8,128)S(1)}, u32[]{:S(2)}, u32[]{:S(2)}) collective-permute-start(f32[128,128]{1,0:T(8,128)S(1)} %get-tuple-element.10), channel_id=1, source_target_pairs={{0,2},{1,3},{2,0},{3,1},{4,6},{5,7},{6,4},{7,5},{8,10},{9,11},{10,... | collective-permute-start | bytes 196616 | tf_op jit(solution)/shard_map/ppermute | solution.py:10
  32.1 15.3 %collective-permute-start.13 = (f32[128,128]{1,0:T(8,128)S(1)}, f32[128,128]{1,0:T(8,128)S(1)}, u32[]{:S(2)}, u32[]{:S(2)}) collective-permute-start(f32[128,128]{1,0:T(8,128)S(1)} %get-tuple-element.8), channel_id=1, source_target_pairs={{0,2},{1,3},{2,0},{3,1},{4,6},{5,7},{6,4},{7,5},{8,10},{9,11},{10,... | collective-permute-start | bytes 196616 | tf_op jit(solution)/shard_map/ppermute | solution.py:10
  37.9 16.8 %collective-permute-start.5 = (f32[128,128]{1,0:T(8,128)S(1)}, f32[128,128]{1,0:T(8,128)S(1)}, u32[]{:S(2)}, u32[]{:S(2)}) collective-permute-start(f32[128,128]{1,0:T(8,128)S(1)} %add.106), channel_id=1, source_target_pairs={{0,4},{1,5},{2,6},{3,7},{4,0},{5,1},{6,2},{7,3},{8,12},{9,13},{10,... | collective-permute-start | bytes 196616 | tf_op jit(solution)/shard_map/ppermute | solution.py:10
  39.9 16.8 %collective-permute-start = (bf16[512,128]{1,0:T(8,128)(2,1)S(1)}, bf16[512,128]{1,0:T(8,128)(2,1)S(1)}, u32[]{:S(2)}, u32[]{:S(2)}) collective-permute-start(bf16[512,128]{1,0:T(8,128)(2,1)S(1)} %copy-done.1), channel_id=1, source_target_pairs={{0,1},{1,0},{2,3},{3,2},{4,5},{5,4},{6,7},{7,6},{8,9},{9,8},{10,11... | collective-permute-start | bytes 393224 | tf_op jit(solution)/shard_map/ppermute | solution.py:10
  41.9 20.3 %collective-permute-start.35 = (f32[128,128]{1,0:T(8,128)S(1)}, f32[128,128]{1,0:T(8,128)S(1)}, u32[]{:S(2)}, u32[]{:S(2)}) collective-permute-start(f32[128,128]{1,0:T(8,128)S(1)} %add.131), channel_id=1, source_target_pairs={{0,4},{1,5},{2,6},{3,7},{4,0},{5,1},{6,2},{7,3},{8,12},{9,13},{10,... | collective-permute-start | bytes 196616 | tf_op jit(solution)/shard_map/ppermute | solution.py:10
  47.3 16.9 %collective-permute-start.27 = (f32[128,128]{1,0:T(8,128)S(1)}, f32[128,128]{1,0:T(8,128)S(1)}, u32[]{:S(2)}, u32[]{:S(2)}) collective-permute-start(f32[128,128]{1,0:T(8,128)S(1)} %add.124), channel_id=1, source_target_pairs={{0,4},{1,5},{2,6},{3,7},{4,0},{5,1},{6,2},{7,3},{8,12},{9,13},{10,... | collective-permute-start | bytes 196616 | tf_op jit(solution)/shard_map/ppermute | solution.py:10
  49.3 18.9 %collective-permute-start.20 = (f32[128,128]{1,0:T(8,128)S(1)}, f32[128,128]{1,0:T(8,128)S(1)}, u32[]{:S(2)}, u32[]{:S(2)}) collective-permute-start(f32[128,128]{1,0:T(8,128)S(1)} %add.118), channel_id=1, source_target_pairs={{0,4},{1,5},{2,6},{3,7},{4,0},{5,1},{6,2},{7,3},{8,12},{9,13},{10,... | collective-permute-start | bytes 196616 | tf_op jit(solution)/shard_map/ppermute | solution.py:10
  54.8 15.4 %collective-permute-start.14 = (f32[128,128]{1,0:T(8,128)S(1)}, f32[128,128]{1,0:T(8,128)S(1)}, u32[]{:S(2)}, u32[]{:S(2)}) collective-permute-start(f32[128,128]{1,0:T(8,128)S(1)} %add.113), channel_id=1, source_target_pairs={{0,4},{1,5},{2,6},{3,7},{4,0},{5,1},{6,2},{7,3},{8,12},{9,13},{10,... | collective-permute-start | bytes 196616 | tf_op jit(solution)/shard_map/ppermute | solution.py:10
  56.7 17.4 %collective-permute-start.9 = (f32[128,128]{1,0:T(8,128)S(1)}, f32[128,128]{1,0:T(8,128)S(1)}, u32[]{:S(2)}, u32[]{:S(2)}) collective-permute-start(f32[128,128]{1,0:T(8,128)S(1)} %add.109), channel_id=1, source_target_pairs={{0,4},{1,5},{2,6},{3,7},{4,0},{5,1},{6,2},{7,3},{8,12},{9,13},{10,... | collective-permute-start | bytes 196616 | tf_op jit(solution)/shard_map/ppermute | solution.py:10
  62.2 13.9 %collective-permute-start.6 = (bf16[128,128]{1,0:T(8,128)(2,1)S(1)}, bf16[128,128]{1,0:T(8,128)(2,1)S(1)}, u32[]{:S(2)}, u32[]{:S(2)}) collective-permute-start(bf16[128,128]{1,0:T(8,128)(2,1)S(1)} %add_convert_fusion.5), channel_id=1, source_target_pairs={{0,8},{1,9},{2,10},{3,11},{4,12},{5,13},{6,14},{7,15},{8,0},{9,1},... | collective-permute-start | bytes 98312 | tf_op jit(solution)/shard_map/ppermute | solution.py:10
  64.2 15.8 %collective-permute-start.36 = (f32[128,128]{1,0:T(8,128)S(1)}, f32[128,128]{1,0:T(8,128)S(1)}, u32[]{:S(2)}, u32[]{:S(2)}) collective-permute-start(f32[128,128]{1,0:T(8,128)S(1)} %add.132), channel_id=1, source_target_pairs={{0,8},{1,9},{2,10},{3,11},{4,12},{5,13},{6,14},{7,15},{8,0},{9,1},... | collective-permute-start | bytes 196616 | tf_op jit(solution)/shard_map/ppermute | solution.py:10
  68.2 15.8 %collective-permute-start.28 = (f32[128,128]{1,0:T(8,128)S(1)}, f32[128,128]{1,0:T(8,128)S(1)}, u32[]{:S(2)}, u32[]{:S(2)}) collective-permute-start(f32[128,128]{1,0:T(8,128)S(1)} %add.125), channel_id=1, source_target_pairs={{0,8},{1,9},{2,10},{3,11},{4,12},{5,13},{6,14},{7,15},{8,0},{9,1},... | collective-permute-start | bytes 196616 | tf_op jit(solution)/shard_map/ppermute | solution.py:10
  70.1 15.8 %collective-permute-start.21 = (f32[128,128]{1,0:T(8,128)S(1)}, f32[128,128]{1,0:T(8,128)S(1)}, u32[]{:S(2)}, u32[]{:S(2)}) collective-permute-start(f32[128,128]{1,0:T(8,128)S(1)} %add.119), channel_id=1, source_target_pairs={{0,8},{1,9},{2,10},{3,11},{4,12},{5,13},{6,14},{7,15},{8,0},{9,1},... | collective-permute-start | bytes 196616 | tf_op jit(solution)/shard_map/ppermute | solution.py:10
  74.1 16.7 %collective-permute-start.15 = (f32[128,128]{1,0:T(8,128)S(1)}, f32[128,128]{1,0:T(8,128)S(1)}, u32[]{:S(2)}, u32[]{:S(2)}) collective-permute-start(f32[128,128]{1,0:T(8,128)S(1)} %add.114), channel_id=1, source_target_pairs={{0,8},{1,9},{2,10},{3,11},{4,12},{5,13},{6,14},{7,15},{8,0},{9,1},... | collective-permute-start | bytes 196616 | tf_op jit(solution)/shard_map/ppermute | solution.py:10
  76.0 16.7 %collective-permute-start.10 = (f32[128,128]{1,0:T(8,128)S(1)}, f32[128,128]{1,0:T(8,128)S(1)}, u32[]{:S(2)}, u32[]{:S(2)}) collective-permute-start(f32[128,128]{1,0:T(8,128)S(1)} %add.110), channel_id=1, source_target_pairs={{0,8},{1,9},{2,10},{3,11},{4,12},{5,13},{6,14},{7,15},{8,0},{9,1},... | collective-permute-start | bytes 196616 | tf_op jit(solution)/shard_map/ppermute | solution.py:10
  80.0 54.9 %collective-permute-start.1 = (bf16[1024,128]{1,0:T(8,128)(2,1)S(1)}, bf16[1024,128]{1,0:T(8,128)(2,1)S(1)}, u32[]{:S(2)}, u32[]{:S(2)}) collective-permute-start(bf16[1024,128]{1,0:T(8,128)(2,1)S(1)} %maximum_select_fusion.3), channel_id=1, source_target_pairs={{0,2},{1,3},{2,0},{3,1},{4,6},{5,7},{6,4},{7,5},{8,10},{9,11},{10,... | collective-permute-start | bytes 786440 | tf_op jit(solution)/shard_map/ppermute | solution.py:10
  84.0 26.4 %collective-permute-start.37 = (f32[128,128]{1,0:T(8,128)S(1)}, f32[128,128]{1,0:T(8,128)S(1)}, u32[]{:S(2)}, u32[]{:S(2)}) collective-permute-start(f32[128,128]{1,0:T(8,128)S(1)} %add.133), channel_id=1, source_target_pairs={{0,16},{1,17},{2,18},{3,19},{4,20},{5,21},{6,22},{7,23},{8,24},{9,... | collective-permute-start | bytes 196616 | tf_op jit(solution)/shard_map/ppermute | solution.py:10
  85.9 30.8 %collective-permute-start.29 = (f32[128,128]{1,0:T(8,128)S(1)}, f32[128,128]{1,0:T(8,128)S(1)}, u32[]{:S(2)}, u32[]{:S(2)}) collective-permute-start(f32[128,128]{1,0:T(8,128)S(1)} %add.126), channel_id=1, source_target_pairs={{0,16},{1,17},{2,18},{3,19},{4,20},{5,21},{6,22},{7,23},{8,24},{9,... | collective-permute-start | bytes 196616 | tf_op jit(solution)/shard_map/ppermute | solution.py:10
  90.8 29.7 %collective-permute-start.22 = (f32[128,128]{1,0:T(8,128)S(1)}, f32[128,128]{1,0:T(8,128)S(1)}, u32[]{:S(2)}, u32[]{:S(2)}) collective-permute-start(f32[128,128]{1,0:T(8,128)S(1)} %add.120), channel_id=1, source_target_pairs={{0,16},{1,17},{2,18},{3,19},{4,20},{5,21},{6,22},{7,23},{8,24},{9,... | collective-permute-start | bytes 196616 | tf_op jit(solution)/shard_map/ppermute | solution.py:10
  106.6 19.9 %collective-permute-start.17 = (bf16[128,128]{1,0:T(8,128)(2,1)S(1)}, bf16[128,128]{1,0:T(8,128)(2,1)S(1)}, u32[]{:S(2)}, u32[]{:S(2)}) collective-permute-start(bf16[128,128]{1,0:T(8,128)(2,1)S(1)} %add_convert_fusion.3), channel_id=1, source_target_pairs={{0,32},{1,33},{2,34},{3,35},{4,36},{5,37},{6,38},{7,39},{8,40},{9,... | collective-permute-start | bytes 98312 | tf_op jit(solution)/shard_map/ppermute | solution.py:10
  110.4 29.0 %collective-permute-start.38 = (f32[128,128]{1,0:T(8,128)S(1)}, f32[128,128]{1,0:T(8,128)S(1)}, u32[]{:S(2)}, u32[]{:S(2)}) collective-permute-start(f32[128,128]{1,0:T(8,128)S(1)} %add.134), channel_id=1, source_target_pairs={{0,32},{1,33},{2,34},{3,35},{4,36},{5,37},{6,38},{7,39},{8,40},{9,... | collective-permute-start | bytes 196616 | tf_op jit(solution)/shard_map/ppermute | solution.py:10
  116.7 24.6 %collective-permute-start.30 = (f32[128,128]{1,0:T(8,128)S(1)}, f32[128,128]{1,0:T(8,128)S(1)}, u32[]{:S(2)}, u32[]{:S(2)}) collective-permute-start(f32[128,128]{1,0:T(8,128)S(1)} %add.127), channel_id=1, source_target_pairs={{0,32},{1,33},{2,34},{3,35},{4,36},{5,37},{6,38},{7,39},{8,40},{9,... | collective-permute-start | bytes 196616 | tf_op jit(solution)/shard_map/ppermute | solution.py:10
  130.6 14.7 %collective-permute-start.24 = (bf16[128,128]{1,0:T(8,128)(2,1)S(1)}, bf16[128,128]{1,0:T(8,128)(2,1)S(1)}, u32[]{:S(2)}, u32[]{:S(2)}) collective-permute-start(bf16[128,128]{1,0:T(8,128)(2,1)S(1)} %add_convert_fusion.2), channel_id=1, source_target_pairs={{0,64},{1,65},{2,66},{3,67},{4,68},{5,69},{6,70},{7,71},{8,72},{9,... | collective-permute-start | bytes 98312 | tf_op jit(solution)/shard_map/ppermute | solution.py:10
  135.0 31.0 %collective-permute-start.2 = (bf16[2048,128]{1,0:T(8,128)(2,1)S(1)}, bf16[2048,128]{1,0:T(8,128)(2,1)S(1)}, u32[]{:S(2)}, u32[]{:S(2)}) collective-permute-start(bf16[2048,128]{1,0:T(8,128)(2,1)S(1)} %maximum_select_fusion.2), channel_id=1, source_target_pairs={{0,4},{1,5},{2,6},{3,7},{4,0},{5,1},{6,2},{7,3},{8,12},{9,13},{10,... | collective-permute-start | bytes 1572872 | tf_op jit(solution)/shard_map/ppermute | solution.py:10
  (21 other events, 266.5 us)
where the time goes:
time: 170 us; the launch traced here: 168 us
  starting transfers between devices  149 us (88%)
  waiting for transfers between devices  12.3 us (7%)
  matrix products  3.23 us (2%)
  local copies, waits for them, and re-layouts  2.06 us (1%)
    ppermute x42, starting transfers between devices, partner(): lax.ppermute(array, axis, [(i, i ^ 1 << distance) for i in range(lax.axis...  149 us
    ppermute x42, waiting for transfers between devices, partner(): lax.ppermute(array, axis, [(i, i ^ 1 << distance) for i in range(lax.axis...  12.3 us
  transfers between devices with their start and end apart: 42, of which 7 were waited for; matrix products, arithmetic and copies ran while one was open for 1% of the time, Pallas kernels for 0%

commit v1 on v0

v1 whole, which is shorter than its diff:
```python
import jax
import jax.numpy as jnp
from jax import lax
from jax.sharding import Mesh, PartitionSpec as P

AXES = ("z", "y_hi", "y_lo", "x", "core")
LEAF = ("x", "core")
PAIR = ("y_lo", "x", "core")
FAR = ("z", "y_hi")


def shards(right_side_block, leaf_rows, bases):
    level_count, _, rank = bases.shape
    width = right_side_block.shape[1]
    pair_devices = lax.axis_size(PAIR)
    far_count = lax.axis_size(FAR)
    slice_rows = rank // pair_devices
    me = lax.axis_index(FAR)
    partial = jnp.einsum(
        "qip,iw->qpw", bases, right_side_block, preferred_element_type=jnp.float32
    )
    outgoing = partial.reshape(level_count, pair_devices, slice_rows, width).swapaxes(0, 1)
    incoming = lax.all_to_all(outgoing, PAIR, 0, 0)
    leaf_sums = incoming.reshape(2, pair_devices // 2, level_count, slice_rows, width).sum(1)
    pair_sums = leaf_sums[0] + leaf_sums[1]
    others = jnp.arange(far_count)
    level_of = jnp.zeros((far_count,), jnp.int32)
    for bit in range(level_count - 1):
        level_of = level_of + ((others ^ me) >> bit > 0).astype(jnp.int32)
    to_far = jnp.zeros((far_count, slice_rows, width), jnp.float32)
    for level in range(1, level_count):
        to_far = jnp.where((level_of == level)[:, None, None], pair_sums[level][None], to_far)
    to_far, late_rhs = lax.optimization_barrier((to_far, right_side_block))
    ring = [
        lax.ppermute(late_rhs, "x", [(i, (i - step) % 4) for i in range(4)]) for step in (1, 3, 2)
    ]
    column = jnp.stack([late_rhs, ring[0], ring[2], ring[1]])
    other = lax.ppermute(column, "core", [(0, 1), (1, 0)])
    core = lax.axis_index("core")
    both = jnp.where(
        core == 0, jnp.stack([column, other], 1), jnp.stack([other, column], 1)
    ).reshape(4, -1, width)
    place = lax.axis_index("x")
    gathered = lax.dynamic_slice_in_dim(
        jnp.concatenate([both, both]), (4 - place) % 4, 4, 0
    ).reshape(-1, width)
    diagonal_part = jnp.dot(leaf_rows, gathered, preferred_element_type=jnp.float32)
    from_far = lax.all_to_all(to_far, FAR, 0, 0)
    siblings = [
        jnp.where((level_of == level)[:, None, None], from_far, 0.0).sum(0)
        for level in range(1, level_count)
    ]
    both = jnp.stack(
        [jnp.stack([leaf_sums[1 - side, 0]] + siblings, 0) for side in range(2)], 0
    ).astype(jnp.bfloat16)
    spread = jnp.broadcast_to(
        both[:, None], (2, pair_devices // 2, level_count, slice_rows, width)
    ).reshape(pair_devices, level_count * slice_rows, width)
    spread = lax.all_to_all(spread, PAIR, 0, 0)
    weights = (
        spread.reshape(pair_devices, level_count, slice_rows, width)
        .swapaxes(0, 1)
        .reshape(level_count, rank, width)
    )
    coupled_product = jnp.einsum(
        "txv,tvu->xu", bases, weights, preferred_element_type=jnp.float32
    )
    return diagonal_part + coupled_product


def solution(mesh):
    fine = Mesh(mesh.devices.reshape(8, 4, 2, 4, 2), AXES)
    in_specs = (P(AXES, None), P(AXES, None), P(None, AXES, None))
    return jax.shard_map(
        shards, mesh=fine, in_specs=in_specs, out_specs=P(AXES, None), check_vma=False
    )
```

time: 170 us -> 64.2 us (0.38)
  the two profiles are of different devices: /device:TPU:2 before, /device:TPU:1 now
where the time goes in v1:
time: 64.2 us; the launch traced here: 63.7 us
  starting transfers between devices  37.5 us (58%)
  waiting for transfers between devices  16.2 us (25%)
  local copies, waits for them, and re-layouts  4.79 us (7%)
  matrix products  3.21 us (5%)
  other arithmetic  1.79 us (3%)
    all_to_all x1, starting transfers between devices, shards(): from_far = lax.all_to_all(to_far, FAR, 0, 0)  11.3 us
    all_to_all x1, starting transfers between devices, shards(): incoming = lax.all_to_all(outgoing, PAIR, 0, 0)  10.2 us
    all_to_all x1, waiting for transfers between devices, shards(): incoming = lax.all_to_all(outgoing, PAIR, 0, 0)  8.42 us
    ppermute x3, starting transfers between devices, shards(): lax.ppermute(late_rhs, 'x', [(i, (i - step) % 4) for i in range(4)])  7.98 us
    all_to_all x1, starting transfers between devices, shards(): spread = lax.all_to_all(spread, PAIR, 0, 0)  5.83 us
    all_to_all x1, waiting for transfers between devices, shards(): spread = lax.all_to_all(spread, PAIR, 0, 0)  4.45 us
    all_to_all x1, waiting for transfers between devices, shards(): from_far = lax.all_to_all(to_far, FAR, 0, 0)  3.31 us
    unnamed x11, local copies, waits for them, and re-layouts  2.45 us
  transfers between devices with their start and end apart: 7, of which 3 were waited for; matrix products, arithmetic and copies ran while one was open for 2% of the time, Pallas kernels for 0%

profile of v1, /device:TPU:1, one launch (start us, length us, event | category | flops | bytes accessed | tf_op | source)
XLA Modules:
  0.0 63.7 jit_solution(2239263657315834844)
XLA Ops:
  0.0 1.1 %copy-done = bf16[6,512,128]{2,1,0:T(8,128)(2,1)S(1)} copy-done((bf16[6,512,128]{2,1,0:T(8,128)(2,1)S(1)}, bf16[6,512,128]{2,1,0:T(8,128)(2,1)}, u32[]{:S(2)}) %copy-start) | copy-done | bytes 786456
  1.1 1.3 %convolution_bitcast_fusion = f32[6,16,8,128]{3,2,1,0:T(8,128)S(1)} fusion(bf16[6,512,128]{2,1,0:T(8,128)(2,1)S(1)} %copy-done, bf16[512,128]{1,0:T(8,128)(2,1)} %param.3), kind=kOutput, calls=%fused_computation.2 | convolution fusion | flops 100663296 | bytes 1310720 | tf_op jit(solution)/shard_map/qip,iw->qpw/dot_general | solution.py:19
  2.4 0.8 %copy.39 = f32[6,16,8,128]{3,2,0,1:T(8,128)} copy(f32[6,16,8,128]{3,2,1,0:T(8,128)S(1)} %convolution_bitcast_fusion) | data formatting | bytes 786432 | tf_op jit(solution)/shard_map/reshape | solution.py:22
  3.2 10.2 %all-to-all-start = ((f32[16,6,8,128]{3,2,1,0:T(8,128)}), f32[16,6,8,128]{3,2,1,0:T(8,128)S(1)}, u32[]{:S(2)}, u32[]{:S(2)}) async-start(f32[16,6,8,128]{3,2,1,0:T(8,128)} %bitcast.73), calls=%async_computation | async-start | bytes 786432 | tf_op jit(solution)/shard_map/all_to_all | solution.py:23
  13.5 8.4 %all-to-all-done = f32[16,6,8,128]{3,2,1,0:T(8,128)S(1)} async-done(((f32[16,6,8,128]{3,2,1,0:T(8,128)}), f32[16,6,8,128]{3,2,1,0:T(8,128)S(1)}, u32[]{:S(2)}, u32[]{:S(2)}) %all-to-all-start) | async-done | bytes 393248 | tf_op jit(solution)/shard_map/all_to_all | solution.py:23
  22.0 0.9 %select_select_fusion = f32[32,8,128]{2,1,0:T(8,128)} fusion(f32[8,128]{1,0:T(8,128)S(1)} %get-tuple-element.19, f32[8,128]{1,0:T(8,128)S(1)} %get-tuple-element.20, f32[8,128]{1,0:T(8,128)S(1)} %get-tuple-element.21, f32[8,128]{1,0:T(8,128)S(1)} %get-tuple-element.22, f32[8,128]{1,0:T(8,128)S(1)} %get-tuple-element.18, ...), kind=kLoop, calls=%fused_computation.19 | loop fusion | flops 163840 | bytes 151712 | tf_op jit(solution)/shard_map/jit(_where)/select_n | solution.py:32
  22.9 11.3 %all-to-all-start.1 = ((f32[32,8,128]{2,1,0:T(8,128)}), f32[32,8,128]{2,1,0:T(8,128)S(1)}, u32[]{:S(2)}, u32[]{:S(2)}) async-start(f32[32,8,128]{2,1,0:T(8,128)} %select_select_fusion), calls=%async_computation.1 | async-start | bytes 262144 | tf_op jit(solution)/shard_map/all_to_all | solution.py:48
  34.2 3.6 %collective-permute-start = (bf16[512,128]{1,0:T(8,128)(2,1)}, bf16[512,128]{1,0:T(8,128)(2,1)S(1)}, u32[]{:S(2)}, u32[]{:S(2)}) collective-permute-start(bf16[512,128]{1,0:T(8,128)(2,1)} %param.3), channel_id=1, source_target_pairs={{0,6},{2,0},{4,2},{6,4},{1,7},{3,1},{5,3},{7,5},{8,14},{10,8},{12,... | collective-permute-start | bytes 393224 | tf_op jit(solution)/shard_map/ppermute | solution.py:35
  37.8 2.0 %collective-permute-start.1 = (bf16[512,128]{1,0:T(8,128)(2,1)}, bf16[512,128]{1,0:T(8,128)(2,1)S(1)}, u32[]{:S(2)}, u32[]{:S(2)}) collective-permute-start(bf16[512,128]{1,0:T(8,128)(2,1)} %param.3), channel_id=1, source_target_pairs={{0,4},{2,6},{4,0},{6,2},{1,5},{3,7},{5,1},{7,3},{8,12},{10,14},{12... | collective-permute-start | bytes 393224 | tf_op jit(solution)/shard_map/ppermute | solution.py:35
  39.8 2.4 %collective-permute-start.2 = (bf16[512,128]{1,0:T(8,128)(2,1)}, bf16[512,128]{1,0:T(8,128)(2,1)S(1)}, u32[]{:S(2)}, u32[]{:S(2)}) collective-permute-start(bf16[512,128]{1,0:T(8,128)(2,1)} %param.3), channel_id=1, source_target_pairs={{0,2},{2,4},{4,6},{6,0},{1,3},{3,5},{5,7},{7,1},{8,10},{10,12},{12... | collective-permute-start | bytes 393224 | tf_op jit(solution)/shard_map/ppermute | solution.py:35
  42.2 3.3 %all-to-all-done.1 = f32[32,8,128]{2,1,0:T(8,128)S(1)} async-done(((f32[32,8,128]{2,1,0:T(8,128)}), f32[32,8,128]{2,1,0:T(8,128)S(1)}, u32[]{:S(2)}, u32[]{:S(2)}) %all-to-all-start.1) | async-done | bytes 131104 | tf_op jit(solution)/shard_map/all_to_all | solution.py:48
  45.5 0.2 select_reduce_fusion
  45.8 0.7 %broadcast_in_dim.125 = bf16[2,8,6,8,128]{4,3,2,1,0:T(8,128)(2,1)} broadcast(bf16[2,6,8,128]{3,2,1,0:T(8,128)(2,1)S(1)} %pad_maximum_fusion.1), dimensions={0,2,3,4} | broadcast | bytes 221184 | tf_op jit(solution)/shard_map/broadcast_in_dim | solution.py:56
  46.5 5.8 %all-to-all-start.2 = ((bf16[16,48,128]{2,1,0:T(8,128)(2,1)}), bf16[16,48,128]{2,1,0:T(8,128)(2,1)S(1)}, u32[]{:S(2)}, u32[]{:S(2)}) async-start(bf16[16,48,128]{2,1,0:T(8,128)(2,1)} %bitcast.26), calls=%async_computation.2 | async-start | bytes 393216 | tf_op jit(solution)/shard_map/all_to_all | solution.py:59
  52.4 0.0 collective-permute-done
  52.4 0.1 fusion.9
  52.5 2.1 %collective-permute-start.3 = (bf16[4,512,128]{2,1,0:T(8,128)(2,1)S(1)}, bf16[4,512,128]{2,1,0:T(8,128)(2,1)S(1)}, u32[]{:S(2)}, u32[]{:S(2)}) collective-permute-start(bf16[4,512,128]{2,1,0:T(8,128)(2,1)S(1)} %get-tuple-element.15), channel_id=1, source_target_pairs={{0,1},{1,0},{2,3},{3,2},{4,5},{5,4},{6,7},{7,6},{8,9},{9,8},{10,11... | collective-permute-start | bytes 1572872 | tf_op jit(solution)/shard_map/ppermute | solution.py:38
  54.7 4.4 %all-to-all-done.2 = bf16[16,48,128]{2,1,0:T(8,128)(2,1)S(1)} async-done(((bf16[16,48,128]{2,1,0:T(8,128)(2,1)}), bf16[16,48,128]{2,1,0:T(8,128)(2,1)S(1)}, u32[]{:S(2)}, u32[]{:S(2)}) %all-to-all-start.2) | async-done | bytes 196640 | tf_op jit(solution)/shard_map/all_to_all | solution.py:59
  59.1 0.4 convolution_bitcast_fusion.1
  59.5 0.1 maximum_select_fusion
  59.6 0.4 fusion.1
  60.0 1.3 %copy-done.1 = bf16[512,4096]{1,0:T(8,128)(2,1)S(1)} copy-done((bf16[512,4096]{1,0:T(8,128)(2,1)S(1)}, bf16[512,4096]{1,0:T(8,128)(2,1)}, u32[]{:S(2)}) %copy-start.1) | copy-done | bytes 4194328
  61.3 1.5 %fusion = f32[512,128]{0,1:T(8,128)S(1)} fusion(f32[128,512]{1,0:T(8,128)S(1)} %convolution_bitcast_fusion.1, bf16[4096,128]{1,0:T(8,128)(2,1)S(1)} %bitcast.75, bf16[512,4096]{1,0:T(8,128)(2,1)S(1)} %copy-done.1), kind=kOutput, calls=%fused_computation.5 | convolution fusion | flops 536936448 | bytes 5767168 | tf_op jit(solution)/shard_map/dot_general | solution.py:47
  62.8 0.8 %copy.23 = f32[512,128]{1,0:T(8,128)} copy(f32[512,128]{0,1:T(8,128)S(1)} %fusion) | data formatting | bytes 524288 | tf_op jit(solution)/shard_map/add | solution.py:68
  (20 shorter events, 0.1 us)
Async XLA Ops:
  0.0 1.1 %copy-start = (bf16[6,512,128]{2,1,0:T(8,128)(2,1)S(1)}, bf16[6,512,128]{2,1,0:T(8,128)(2,1)}, u32[]{:S(2)}) copy-start(bf16[6,512,128]{2,1,0:T(8,128)(2,1)} %param.5) | copy-start | bytes 2359300
  0.0 52.4 %copy-start.2 = (bf16[512,128]{1,0:T(8,128)(2,1)S(1)}, bf16[512,128]{1,0:T(8,128)(2,1)}, u32[]{:S(2)}) copy-start(bf16[512,128]{1,0:T(8,128)(2,1)} %param.3) | copy-start | bytes 393220
  3.2 18.7 %all-to-all-start = ((f32[16,6,8,128]{3,2,1,0:T(8,128)}), f32[16,6,8,128]{3,2,1,0:T(8,128)S(1)}, u32[]{:S(2)}, u32[]{:S(2)}) async-start(f32[16,6,8,128]{3,2,1,0:T(8,128)} %bitcast.73), calls=%async_computation | async-start | bytes 786432 | tf_op jit(solution)/shard_map/all_to_all | solution.py:23
  22.9 22.7 %all-to-all-start.1 = ((f32[32,8,128]{2,1,0:T(8,128)}), f32[32,8,128]{2,1,0:T(8,128)S(1)}, u32[]{:S(2)}, u32[]{:S(2)}) async-start(f32[32,8,128]{2,1,0:T(8,128)} %select_select_fusion), calls=%async_computation.1 | async-start | bytes 262144 | tf_op jit(solution)/shard_map/all_to_all | solution.py:48
  34.2 18.2 %collective-permute-start = (bf16[512,128]{1,0:T(8,128)(2,1)}, bf16[512,128]{1,0:T(8,128)(2,1)S(1)}, u32[]{:S(2)}, u32[]{:S(2)}) collective-permute-start(bf16[512,128]{1,0:T(8,128)(2,1)} %param.3), channel_id=1, source_target_pairs={{0,6},{2,0},{4,2},{6,4},{1,7},{3,1},{5,3},{7,5},{8,14},{10,8},{12,... | collective-permute-start | bytes 393224 | tf_op jit(solution)/shard_map/ppermute | solution.py:35
  37.8 14.6 %collective-permute-start.1 = (bf16[512,128]{1,0:T(8,128)(2,1)}, bf16[512,128]{1,0:T(8,128)(2,1)S(1)}, u32[]{:S(2)}, u32[]{:S(2)}) collective-permute-start(bf16[512,128]{1,0:T(8,128)(2,1)} %param.3), channel_id=1, source_target_pairs={{0,4},{2,6},{4,0},{6,2},{1,5},{3,7},{5,1},{7,3},{8,12},{10,14},{12... | collective-permute-start | bytes 393224 | tf_op jit(solution)/shard_map/ppermute | solution.py:35
  39.8 12.6 %collective-permute-start.2 = (bf16[512,128]{1,0:T(8,128)(2,1)}, bf16[512,128]{1,0:T(8,128)(2,1)S(1)}, u32[]{:S(2)}, u32[]{:S(2)}) collective-permute-start(bf16[512,128]{1,0:T(8,128)(2,1)} %param.3), channel_id=1, source_target_pairs={{0,2},{2,4},{4,6},{6,0},{1,3},{3,5},{5,7},{7,1},{8,10},{10,12},{12... | collective-permute-start | bytes 393224 | tf_op jit(solution)/shard_map/ppermute | solution.py:35
  46.5 12.6 %all-to-all-start.2 = ((bf16[16,48,128]{2,1,0:T(8,128)(2,1)}), bf16[16,48,128]{2,1,0:T(8,128)(2,1)S(1)}, u32[]{:S(2)}, u32[]{:S(2)}) async-start(bf16[16,48,128]{2,1,0:T(8,128)(2,1)} %bitcast.26), calls=%async_computation.2 | async-start | bytes 393216 | tf_op jit(solution)/shard_map/all_to_all | solution.py:59
  52.5 7.0 %collective-permute-start.3 = (bf16[4,512,128]{2,1,0:T(8,128)(2,1)S(1)}, bf16[4,512,128]{2,1,0:T(8,128)(2,1)S(1)}, u32[]{:S(2)}, u32[]{:S(2)}) collective-permute-start(bf16[4,512,128]{2,1,0:T(8,128)(2,1)S(1)} %get-tuple-element.15), channel_id=1, source_target_pairs={{0,1},{1,0},{2,3},{3,2},{4,5},{5,4},{6,7},{7,6},{8,9},{9,8},{10,11... | collective-permute-start | bytes 1572872 | tf_op jit(solution)/shard_map/ppermute | solution.py:38
  59.1 2.2 %copy-start.1 = (bf16[512,4096]{1,0:T(8,128)(2,1)S(1)}, bf16[512,4096]{1,0:T(8,128)(2,1)}, u32[]{:S(2)}) copy-start(bf16[512,4096]{1,0:T(8,128)(2,1)} %param.4) | copy-start | bytes 12582916

commit v2 on v0

v2 whole, which is shorter than its diff:
```python
import jax
import jax.numpy as jnp
from jax import lax
from jax.experimental import pallas as pl
from jax.experimental.pallas import tpu as pltpu
from jax.sharding import PartitionSpec as P

CHIPS = 4
LEAF_DEVS = 2 * CHIPS
PAIR_DEVS = 2 * LEAF_DEVS
LATE_PAIR = 30
LATE_PLACE = 6
VMEM = pl.BlockSpec(memory_space=pltpu.VMEM)


def call(kernel, outs, flops, *args):
    return pl.pallas_call(
        kernel,
        out_shape=outs,
        in_specs=[VMEM] * len(args),
        out_specs=jax.tree.map(lambda _: VMEM, outs),
        compiler_params=pltpu.CompilerParams(vmem_limit_bytes=16 << 20),
        cost_estimate=pl.CostEstimate(
            flops=flops,
            bytes_accessed=flops // 250 + sum(a.size * a.dtype.itemsize for a in args),
            transcendentals=0,
        ),
        name=kernel.__name__,
    )(*args)


def far_place():
    return lax.div(lax.axis_index("leaf"), PAIR_DEVS) ^ LATE_PAIR


def outer_block(place, bit):
    return ((place >> bit) ^ 1) << bit


def send_far(incoming_ref, far_ref, near_ref):
    sums = [incoming_ref[0], incoming_ref[LEAF_DEVS]]
    for k in range(1, LEAF_DEVS):
        sums[0] += incoming_ref[k]
        sums[1] += incoming_ref[LEAF_DEVS + k]
    both = sums[0] + sums[1]
    near_ref[0] = sums[1][0]
    near_ref[1] = sums[0][0]
    place = far_place()
    far_ref[place] = both[0]
    for bit in range(both.shape[0] - 1):
        span = 1 << bit
        far_ref[pl.ds(outer_block(place, bit), span)] = jnp.broadcast_to(
            both[bit + 1], (span,) + both.shape[1:]
        )


def gather_siblings(far_ref, near_ref, spread_ref):
    place = far_place()
    pieces = []
    for bit in range(far_ref.shape[0].bit_length() - 1):
        pieces.append(far_ref[pl.ds(outer_block(place, bit), 1 << bit)].sum(0))
    for side in range(2):
        block = jnp.concatenate([near_ref[side]] + pieces, 0).astype(spread_ref.dtype)
        for k in range(LEAF_DEVS):
            spread_ref[side * LEAF_DEVS + k] = block


def place_in_leaf():
    position = lax.rem(lax.axis_index("leaf"), LEAF_DEVS)
    return lax.div(position, 2), lax.rem(position, 2)


def columns(rows_ref, block, count):
    points = rows_ref.shape[0]
    start = pl.multiple_of(lax.rem(block, LEAF_DEVS) * points, points)
    return rows_ref[:, pl.ds(start, count * points)]


def early_blocks(rows_ref, own_ref, side_ref, opposite_ref, out_ref, rest_ref):
    chip, core = place_in_leaf()
    total = jnp.zeros(out_ref.shape, jnp.float32)
    for turn, block in ((0, own_ref), (1 + 2 * core, side_ref), (2, opposite_ref)):
        total += jnp.dot(
            columns(rows_ref, 2 * (chip + turn), 2),
            block[...],
            preferred_element_type=jnp.float32,
        )
    out_ref[...] = total
    rest_ref[...] = columns(rows_ref, 2 * (chip + 3 - 2 * core), 2)


def last_block(rest_ref, other_ref, early_ref, out_ref):
    out_ref[...] = early_ref[...] + jnp.dot(
        rest_ref[...], other_ref[...], preferred_element_type=jnp.float32
    )


def finish(bases_ref, spread_ref, diagonal_ref, out_ref):
    level_count = bases_ref.shape[0]
    total = diagonal_ref[...]
    slices = [spread_ref[k].astype(jnp.float32) for k in range(PAIR_DEVS)]
    deep = slices[0].shape[0] // level_count
    for level in range(0, level_count, 2):
        weights = jnp.concatenate(
            [s[l * deep : (l + 1) * deep] for l in (level, level + 1) for s in slices], 0
        ).astype(bases_ref.dtype)
        factor = jnp.concatenate([bases_ref[level], bases_ref[level + 1]], 1)
        total += jnp.dot(factor, weights, preferred_element_type=jnp.float32)
    out_ref[...] = total


def shards(right_side_block, leaf_rows, bases):
    level_count, points, rank = bases.shape
    width = right_side_block.shape[1]
    device_count = lax.axis_size("leaf")
    pair_count = device_count // PAIR_DEVS
    slice_rows = rank // PAIR_DEVS
    near = [
        [p * PAIR_DEVS + (k ^ LATE_PLACE) for k in range(PAIR_DEVS)] for p in range(pair_count)
    ]
    far = [
        [(k ^ LATE_PAIR) * PAIR_DEVS + m for k in range(pair_count)] for m in range(PAIR_DEVS)
    ]
    f32 = lambda *shape: jax.ShapeDtypeStruct(shape, jnp.float32)

    partial = jnp.einsum(
        "qip,iw->qpw", bases, right_side_block, preferred_element_type=jnp.float32
    )
    outgoing = partial.reshape(level_count, PAIR_DEVS, slice_rows, width).swapaxes(0, 1)
    incoming = lax.all_to_all(outgoing, "leaf", 0, 0, axis_index_groups=near)

    swap = [(i, i ^ 1) for i in range(device_count)]
    twin = lax.ppermute(right_side_block, "leaf", swap)
    own = jnp.where(
        lax.axis_index("leaf") % 2 == 0,
        jnp.concatenate([right_side_block, twin]),
        jnp.concatenate([twin, right_side_block]),
    )
    to_far, beside = call(
        send_far, (f32(pair_count, slice_rows, width), f32(2, slice_rows, width)), 0, incoming
    )
    to_far, own = lax.optimization_barrier((to_far, own))
    from_far = lax.all_to_all(to_far, "leaf", 0, 0, axis_index_groups=far)
    leaf_of = lambda i: i // LEAF_DEVS * LEAF_DEVS
    beyond = [
        lax.ppermute(
            own, "leaf", [(i, leaf_of(i) + (i + step[i % 2]) % LEAF_DEVS) for i in range(device_count)]
        )
        for step in ((-2, 2), (4, 4))
    ]
    spread = call(
        gather_siblings,
        jax.ShapeDtypeStruct((PAIR_DEVS, level_count * slice_rows, width), bases.dtype),
        0,
        from_far,
        beside,
    )
    spread = lax.all_to_all(spread, "leaf", 0, 0, axis_index_groups=near)

    side, opposite = lax.optimization_barrier(tuple(beyond))
    other = lax.ppermute(side, "leaf", swap)
    early, rest = call(
        early_blocks,
        (f32(points, width), jax.ShapeDtypeStruct((points, 2 * points), bases.dtype)),
        0 * leaf_rows.size * width,
        leaf_rows,
        own,
        side,
        opposite,
    )
    product = call(last_block, f32(points, width), 0, rest, other, early)
    return call(finish, f32(points, width), bases.size * width, bases, spread, product)


def solution(mesh):
    in_specs = (P("leaf", None), P("leaf", None), P(None, "leaf", None))
    return jax.shard_map(
        shards, mesh=mesh, in_specs=in_specs, out_specs=P("leaf", None), check_vma=False
    )
```

time: 170 us -> 57.6 us (0.34)
  the two profiles are of different devices: /device:TPU:2 before, /device:TPU:1 now
where the time goes in v2:
time: 57.6 us; the launch traced here: 56.7 us
  starting transfers between devices  41.6 us (72%)
  waiting for transfers between devices  5.45 us (9%)
  Pallas kernels  3.94 us (7%)
  local copies, waits for them, and re-layouts  2.96 us (5%)
  matrix products  1.54 us (3%)
  other arithmetic  1.05 us (2%)
    all_to_all x1, starting transfers between devices, shards(): from_far = lax.all_to_all(to_far, 'leaf', 0, 0, axis_index_groups=far)  14 us
    all_to_all x1, starting transfers between devices, shards(): incoming = lax.all_to_all(outgoing, 'leaf', 0, 0, axis_index_groups=near)  11 us
    ppermute x2, starting transfers between devices, shards(): lax.ppermute(own, 'leaf', [(i, leaf_of(i) + (i + step[i % 2]) % LEAF_DEVS...  6.04 us
    all_to_all x1, starting transfers between devices, shards(): spread = lax.all_to_all(spread, 'leaf', 0, 0, axis_index_groups=near)  5.95 us
    pallas_call x5, Pallas kernels, call(): pl.pallas_call(kernel, out_shape=outs, in_specs=[VMEM] * len(args), out_s...  3.94 us
    all_to_all x1, waiting for transfers between devices, shards(): incoming = lax.all_to_all(outgoing, 'leaf', 0, 0, axis_index_groups=near)  2.94 us
    ppermute x1, starting transfers between devices, shards(): other = lax.ppermute(side, 'leaf', swap)  2.35 us
    ppermute x1, starting transfers between devices, shards(): twin = lax.ppermute(right_side_block, 'leaf', swap)  2.26 us
  transfers between devices with their start and end apart: 7, of which 3 were waited for; matrix products, arithmetic and copies ran while one was open for 2% of the time, Pallas kernels for 4%

profile of v2, /device:TPU:1, one launch (start us, length us, event | category | flops | bytes accessed | tf_op | source)
XLA Modules:
  0.0 56.7 jit_solution(9572719769258093915)
XLA Ops:
  0.0 1.5 %convolution_bitcast_fusion = f32[6,16,8,128]{3,2,1,0:T(8,128)S(1)} fusion(bf16[6,512,128]{2,1,0:T(8,128)(2,1)} %bases_ref.1, bf16[512,128]{1,0:T(8,128)(2,1)} %param.3), kind=kOutput, calls=%fused_computation | convolution fusion | flops 100663296 | bytes 1310720 | tf_op jit(solution)/shard_map/qip,iw->qpw/dot_general | solution.py:126
  1.5 0.8 %copy.9 = f32[6,16,8,128]{3,2,0,1:T(8,128)} copy(f32[6,16,8,128]{3,2,1,0:T(8,128)S(1)} %convolution_bitcast_fusion) | data formatting | bytes 786432 | tf_op jit(solution)/shard_map/reshape | solution.py:129
  2.3 11.0 %all-to-all-start = ((f32[16,6,8,128]{3,2,1,0:T(8,128)}), f32[16,6,8,128]{3,2,1,0:T(8,128)S(1)}, u32[]{:S(2)}, u32[]{:S(2)}) async-start(f32[16,6,8,128]{3,2,1,0:T(8,128)} %bitcast.8), calls=%async_computation | async-start | bytes 786432 | tf_op jit(solution)/shard_map/all_to_all | solution.py:130
  13.4 2.3 %collective-permute-start = (bf16[512,128]{1,0:T(8,128)(2,1)}, bf16[512,128]{1,0:T(8,128)(2,1)S(1)}, u32[]{:S(2)}, u32[]{:S(2)}) collective-permute-start(bf16[512,128]{1,0:T(8,128)(2,1)} %param.3), channel_id=1, source_target_pairs={{0,1},{1,0},{2,3},{3,2},{4,5},{5,4},{6,7},{7,6},{8,9},{9,8},{10,11... | collective-permute-start | bytes 393224 | tf_op jit(solution)/shard_map/ppermute | solution.py:133
  15.6 1.2 %collective-permute-done = bf16[512,128]{1,0:T(8,128)(2,1)S(1)} collective-permute-done((bf16[512,128]{1,0:T(8,128)(2,1)}, bf16[512,128]{1,0:T(8,128)(2,1)S(1)}, u32[]{:S(2)}, u32[]{:S(2)}) %collective-permute-start) | collective-permute-done | bytes 131104 | tf_op jit(solution)/shard_map/ppermute | solution.py:133
  16.8 1.0 %maximum_select_fusion.own_ref = bf16[1024,128]{1,0:T(8,128)(2,1)S(1)} fusion(bf16[512,128]{1,0:T(8,128)(2,1)S(1)} %collective-permute-done, bf16[512,128]{1,0:T(8,128)(2,1)} %param.3, pred[]{:T(512)S(6)} %eq.5), kind=kLoop, calls=%fused_computation.2 | loop fusion | flops 1179648 | bytes 524289 | tf_op jit(solution)/shard_map/jit(_where)/select_n | solution.py:134
  17.9 0.0 copy-start.1
  17.9 2.9 %all-to-all-done.incoming_ref = f32[16,6,8,128]{3,2,1,0:T(8,128)S(1)} async-done(((f32[16,6,8,128]{3,2,1,0:T(8,128)}), f32[16,6,8,128]{3,2,1,0:T(8,128)S(1)}, u32[]{:S(2)}, u32[]{:S(2)}) %all-to-all-start) | async-done | bytes 393248 | tf_op jit(solution)/shard_map/all_to_all | solution.py:130
  20.8 0.7 %send_far.1 = (f32[32,8,128]{2,1,0:T(8,128)}, f32[2,8,128]{2,1,0:T(8,128)S(1)}) custom-call(f32[16,6,8,128]{3,2,1,0:T(8,128)S(1)} %all-to-all-done.incoming_ref), custom_call_target="tpu_custom_call" | custom-call | bytes 393216 | tf_op jit(solution)/shard_map/send_far/pallas_call | solution.py:17
  21.5 14.0 %all-to-all-start.1 = ((f32[32,8,128]{2,1,0:T(8,128)}), f32[32,8,128]{2,1,0:T(8,128)S(1)}, u32[]{:S(2)}, u32[]{:S(2)}) async-start(f32[32,8,128]{2,1,0:T(8,128)} %get-tuple-element.14), calls=%async_computation.1 | async-start | bytes 262144 | tf_op jit(solution)/shard_map/all_to_all | solution.py:143
  35.5 1.9 %collective-permute-start.1 = (bf16[1024,128]{1,0:T(8,128)(2,1)S(1)}, bf16[1024,128]{1,0:T(8,128)(2,1)S(1)}, u32[]{:S(2)}, u32[]{:S(2)}) collective-permute-start(bf16[1024,128]{1,0:T(8,128)(2,1)S(1)} %maximum_select_fusion.own_ref), channel_id=1, source_target_pairs={{0,6},{1,3},{2,0},{3,5},{4,2},{5,7},{6,4},{7,1},{8,14},{9,11},{10,... | collective-permute-start | bytes 786440 | tf_op jit(solution)/shard_map/ppermute | solution.py:146
  37.4 4.1 %collective-permute-start.2 = (bf16[1024,128]{1,0:T(8,128)(2,1)S(1)}, bf16[1024,128]{1,0:T(8,128)(2,1)S(1)}, u32[]{:S(2)}, u32[]{:S(2)}) collective-permute-start(bf16[1024,128]{1,0:T(8,128)(2,1)S(1)} %maximum_select_fusion.own_ref), channel_id=1, source_target_pairs={{0,4},{1,5},{2,6},{3,7},{4,0},{5,1},{6,2},{7,3},{8,12},{9,13},{10,... | collective-permute-start | bytes 786440 | tf_op jit(solution)/shard_map/ppermute | solution.py:146
  41.5 0.0 all-to-all-done.1.far_ref
  41.6 0.7 %gather_siblings.1 = bf16[16,48,128]{2,1,0:T(8,128)(2,1)} custom-call(f32[32,8,128]{2,1,0:T(8,128)S(1)} %all-to-all-done.1.far_ref, f32[2,8,128]{2,1,0:T(8,128)S(1)} %get-tuple-element.15.near_ref), custom_call_target="tpu_custom_call" | custom-call | bytes 139264 | tf_op jit(solution)/shard_map/gather_siblings/pallas_call | solution.py:17
  42.3 5.9 %all-to-all-start.2 = ((bf16[16,48,128]{2,1,0:T(8,128)(2,1)}), bf16[16,48,128]{2,1,0:T(8,128)(2,1)S(1)}, u32[]{:S(2)}, u32[]{:S(2)}) async-start(bf16[16,48,128]{2,1,0:T(8,128)(2,1)} %gather_siblings.1), calls=%async_computation.2 | async-start | bytes 393216 | tf_op jit(solution)/shard_map/all_to_all | solution.py:158
  48.2 1.3 %collective-permute-done.1.side_ref = bf16[1024,128]{1,0:T(8,128)(2,1)S(1)} collective-permute-done((bf16[1024,128]{1,0:T(8,128)(2,1)S(1)}, bf16[1024,128]{1,0:T(8,128)(2,1)S(1)}, u32[]{:S(2)}, u32[]{:S(2)}) %collective-permute-start.1) | collective-permute-done | bytes 262176 | tf_op jit(solution)/shard_map/ppermute | solution.py:146
  49.5 2.3 %collective-permute-start.3 = (bf16[1024,128]{1,0:T(8,128)(2,1)S(1)}, bf16[1024,128]{1,0:T(8,128)(2,1)S(1)}, u32[]{:S(2)}, u32[]{:S(2)}) collective-permute-start(bf16[1024,128]{1,0:T(8,128)(2,1)S(1)} %collective-permute-done.1.side_ref), channel_id=1, source_target_pairs={{0,1},{1,0},{2,3},{3,2},{4,5},{5,4},{6,7},{7,6},{8,9},{9,8},{10,11... | collective-permute-start | bytes 786440 | tf_op jit(solution)/shard_map/ppermute | solution.py:161
  51.9 0.0 copy-start
  51.9 2.2 %copy-done = bf16[512,4096]{1,0:T(8,128)(2,1)S(1)} copy-done((bf16[512,4096]{1,0:T(8,128)(2,1)S(1)}, bf16[512,4096]{1,0:T(8,128)(2,1)}, u32[]{:S(2)}) %copy-start) | copy-done | bytes 4194328
  54.1 1.0 %early_blocks.1 = (f32[512,128]{1,0:T(8,128)S(1)}, bf16[512,1024]{1,0:T(8,128)(2,1)S(1)}) custom-call(bf16[512,4096]{1,0:T(8,128)(2,1)S(1)} %copy-done, bf16[1024,128]{1,0:T(8,128)(2,1)S(1)} %maximum_select_fusion.own_ref, bf16[1024,128]{1,0:T(8,128)(2,1)S(1)} %collective-permute-done.1.side_ref, bf16[1024,128]{1,0:T(8,128)(2,1)S(1)} %collective-permute-done.2.opposite_ref), custom_call_target="tpu_custom_call" | custom-call | bytes 4980736 | tf_op jit(solution)/shard_map/early_blocks/pallas_call | solution.py:17
  55.1 0.0 collective-permute-done.3.other_ref
  55.1 0.4 last_block.1.diagonal_ref
  55.6 0.0 all-to-all-done.2.spread_ref
  55.6 1.1 %finish.1 = f32[512,128]{1,0:T(8,128)} custom-call(bf16[6,512,128]{2,1,0:T(8,128)(2,1)S(1)} %copy-done.1, bf16[16,48,128]{2,1,0:T(8,128)(2,1)S(1)} %all-to-all-done.2.spread_ref, f32[512,128]{1,0:T(8,128)S(1)} %last_block.1.diagonal_ref), custom_call_target="tpu_custom_call" | custom-call | flops 50331648 | bytes 1446510 | tf_op jit(solution)/shard_map/finish/pallas_call | solution.py:17
  (2 shorter events, 0.0 us)
Async XLA Ops:
  2.3 18.5 %all-to-all-start = ((f32[16,6,8,128]{3,2,1,0:T(8,128)}), f32[16,6,8,128]{3,2,1,0:T(8,128)S(1)}, u32[]{:S(2)}, u32[]{:S(2)}) async-start(f32[16,6,8,128]{3,2,1,0:T(8,128)} %bitcast.8), calls=%async_computation | async-start | bytes 786432 | tf_op jit(solution)/shard_map/all_to_all | solution.py:130
  13.4 3.4 %collective-permute-start = (bf16[512,128]{1,0:T(8,128)(2,1)}, bf16[512,128]{1,0:T(8,128)(2,1)S(1)}, u32[]{:S(2)}, u32[]{:S(2)}) collective-permute-start(bf16[512,128]{1,0:T(8,128)(2,1)} %param.3), channel_id=1, source_target_pairs={{0,1},{1,0},{2,3},{3,2},{4,5},{5,4},{6,7},{7,6},{8,9},{9,8},{10,11... | collective-permute-start | bytes 393224 | tf_op jit(solution)/shard_map/ppermute | solution.py:133
  17.9 37.7 %copy-start.1 = (bf16[6,512,128]{2,1,0:T(8,128)(2,1)S(1)}, bf16[6,512,128]{2,1,0:T(8,128)(2,1)}, u32[]{:S(2)}) copy-start(bf16[6,512,128]{2,1,0:T(8,128)(2,1)} %bases_ref.1) | copy-start | bytes 2359300
  21.5 20.1 %all-to-all-start.1 = ((f32[32,8,128]{2,1,0:T(8,128)}), f32[32,8,128]{2,1,0:T(8,128)S(1)}, u32[]{:S(2)}, u32[]{:S(2)}) async-start(f32[32,8,128]{2,1,0:T(8,128)} %get-tuple-element.14), calls=%async_computation.1 | async-start | bytes 262144 | tf_op jit(solution)/shard_map/all_to_all | solution.py:143
  35.5 14.1 %collective-permute-start.1 = (bf16[1024,128]{1,0:T(8,128)(2,1)S(1)}, bf16[1024,128]{1,0:T(8,128)(2,1)S(1)}, u32[]{:S(2)}, u32[]{:S(2)}) collective-permute-start(bf16[1024,128]{1,0:T(8,128)(2,1)S(1)} %maximum_select_fusion.own_ref), channel_id=1, source_target_pairs={{0,6},{1,3},{2,0},{3,5},{4,2},{5,7},{6,4},{7,1},{8,14},{9,11},{10,... | collective-permute-start | bytes 786440 | tf_op jit(solution)/shard_map/ppermute | solution.py:146
  37.4 12.1 %collective-permute-start.2 = (bf16[1024,128]{1,0:T(8,128)(2,1)S(1)}, bf16[1024,128]{1,0:T(8,128)(2,1)S(1)}, u32[]{:S(2)}, u32[]{:S(2)}) collective-permute-start(bf16[1024,128]{1,0:T(8,128)(2,1)S(1)} %maximum_select_fusion.own_ref), channel_id=1, source_target_pairs={{0,4},{1,5},{2,6},{3,7},{4,0},{5,1},{6,2},{7,3},{8,12},{9,13},{10,... | collective-permute-start | bytes 786440 | tf_op jit(solution)/shard_map/ppermute | solution.py:146
  42.3 13.3 %all-to-all-start.2 = ((bf16[16,48,128]{2,1,0:T(8,128)(2,1)}), bf16[16,48,128]{2,1,0:T(8,128)(2,1)S(1)}, u32[]{:S(2)}, u32[]{:S(2)}) async-start(bf16[16,48,128]{2,1,0:T(8,128)(2,1)} %gather_siblings.1), calls=%async_computation.2 | async-start | bytes 393216 | tf_op jit(solution)/shard_map/all_to_all | solution.py:158
  49.5 5.6 %collective-permute-start.3 = (bf16[1024,128]{1,0:T(8,128)(2,1)S(1)}, bf16[1024,128]{1,0:T(8,128)(2,1)S(1)}, u32[]{:S(2)}, u32[]{:S(2)}) collective-permute-start(bf16[1024,128]{1,0:T(8,128)(2,1)S(1)} %collective-permute-done.1.side_ref), channel_id=1, source_target_pairs={{0,1},{1,0},{2,3},{3,2},{4,5},{5,4},{6,7},{7,6},{8,9},{9,8},{10,11... | collective-permute-start | bytes 786440 | tf_op jit(solution)/shard_map/ppermute | solution.py:161
  51.9 2.2 %copy-start = (bf16[512,4096]{1,0:T(8,128)(2,1)S(1)}, bf16[512,4096]{1,0:T(8,128)(2,1)}, u32[]{:S(2)}) copy-start(bf16[512,4096]{1,0:T(8,128)(2,1)} %rows_ref.1) | copy-start | bytes 12582916

commit v3 on v2

--- a/solution.py
+++ b/solution.py
@@ -126,9 +126,26 @@
     partial = jnp.einsum(
         "qip,iw->qpw", bases, right_side_block, preferred_element_type=jnp.float32
     )
-    outgoing = partial.reshape(level_count, PAIR_DEVS, slice_rows, width).swapaxes(0, 1)
-    incoming = lax.all_to_all(outgoing, "leaf", 0, 0, axis_index_groups=near)
-
+    largest = jnp.max(jnp.abs(partial), axis=(1, 2))
+    power = 14.0 - jnp.ceil(jnp.log2(jnp.maximum(largest, 1e-30)))
+    scaled = (partial * jnp.exp2(power)[:, None, None]).astype(jnp.float16)
+    powers = jnp.broadcast_to(
+        jnp.pad(power, (0, slice_rows - level_count))[None, :, None],
+        (PAIR_DEVS, slice_rows, width),
+    ).astype(jnp.float16)
+    outgoing = scaled.reshape(level_count, PAIR_DEVS, slice_rows, width).swapaxes(0, 1)
+    outgoing = jnp.concatenate(
+        [outgoing.reshape(PAIR_DEVS, level_count * slice_rows, width), powers], 1
+    )
+    received = lax.all_to_all(outgoing, "leaf", 0, 0, axis_index_groups=near)
+    received = received.astype(jnp.float32)
+    undo = jnp.exp2(-received[:, level_count * slice_rows :][:, :level_count])
+    incoming = (
+        received[:, : level_count * slice_rows].reshape(
+            PAIR_DEVS, level_count, slice_rows, width
+        )
+        * undo[:, :, None, :]
+    )
     swap = [(i, i ^ 1) for i in range(device_count)]
     twin = lax.ppermute(right_side_block, "leaf", swap)
     own = jnp.where(
@@ -146,7 +163,7 @@
         lax.ppermute(
             own, "leaf", [(i, leaf_of(i) + (i + step[i % 2]) % LEAF_DEVS) for i in range(device_count)]
         )
-        for step in ((-2, 2), (4, 4))
+        for step in ((4, 4), (-2, 2))
     ]
     spread = call(
         gather_siblings,
@@ -157,7 +174,7 @@
     )
     spread = lax.all_to_all(spread, "leaf", 0, 0, axis_index_groups=near)
 
-    side, opposite = lax.optimization_barrier(tuple(beyond))
+    opposite, side = lax.optimization_barrier(tuple(beyond))
     other = lax.ppermute(side, "leaf", swap)
     early, rest = call(
         early_blocks,

time: 57.6 us -> 56 us (0.972)
  other arithmetic: 1.05 us -> 2.16 us
  waiting for transfers between devices: 5.45 us -> 4.5 us
  local copies, waits for them, and re-layouts: 2.96 us -> 2.19 us
  starting transfers between devices: 41.6 us -> 40.9 us
    all_to_all x1, waiting for transfers between devices: 2.94 us -> 1.2 us  [shards(): received = lax.all_to_all(outgoing, 'leaf', 0, 0, axis_index_groups=near)]
    concatenate x0 -> x2, other arithmetic: none -> 0.89 us  [shards(): jnp.concatenate([outgoing.reshape(PAIR_DEVS, level_count * slice_rows, wi...]
    reshape x1 -> x0, local copies, waits for them, and re-layouts: 0.77 us -> none  [shards(): partial.reshape(level_count, PAIR_DEVS, slice_rows, width).swapaxes(0, 1)]
    ppermute x2, waiting for transfers between devices: 1.33 us -> 1.96 us  [shards(): lax.ppermute(own, 'leaf', [(i, leaf_of(i) + (i + step[i % 2]) % LEAF_DEVS...]
  transfers between devices with their start and end apart: 7 -> 7, of which waited for: 3 -> 4; matrix products, arithmetic and copies ran while one was open for 2% -> 2% of each run, Pallas kernels for 4% -> 4%
where the time goes in v3:
time: 56 us; the launch traced here: 55.5 us
  starting transfers between devices  40.9 us (73%)
  waiting for transfers between devices  4.5 us (8%)
  Pallas kernels  3.93 us (7%)
  local copies, waits for them, and re-layouts  2.19 us (4%)
  other arithmetic  2.16 us (4%)
  matrix products  1.63 us (3%)
    all_to_all x1, starting transfers between devices, shards(): from_far = lax.all_to_all(to_far, 'leaf', 0, 0, axis_index_groups=far)  14 us
    all_to_all x1, starting transfers between devices, shards(): received = lax.all_to_all(outgoing, 'leaf', 0, 0, axis_index_groups=near)  11 us
    all_to_all x1, starting transfers between devices, shards(): spread = lax.all_to_all(spread, 'leaf', 0, 0, axis_index_groups=near)  6.03 us
    ppermute x2, starting transfers between devices, shards(): lax.ppermute(own, 'leaf', [(i, leaf_of(i) + (i + step[i % 2]) % LEAF_DEVS...  5.73 us
    pallas_call x5, Pallas kernels, call(): pl.pallas_call(kernel, out_shape=outs, in_specs=[VMEM] * len(args), out_s...  3.93 us
    ppermute x1, starting transfers between devices, shards(): twin = lax.ppermute(right_side_block, 'leaf', swap)  2.26 us
    unnamed x4, local copies, waits for them, and re-layouts  2.19 us
    ppermute x2, waiting for transfers between devices, shards(): lax.ppermute(own, 'leaf', [(i, leaf_of(i) + (i + step[i % 2]) % LEAF_DEVS...  1.96 us
  transfers between devices with their start and end apart: 7, of which 4 were waited for; matrix products, arithmetic and copies ran while one was open for 2% of the time, Pallas kernels for 4%

profile of v3, /device:TPU:1, one launch (start us, length us, event | category | flops | bytes accessed | tf_op | source)
XLA Modules:
  0.0 55.5 jit_solution(16618188663231349922)
XLA Ops:
  0.0 1.6 %abs_reduce_fusion = (f32[6]{0:T(128)S(1)}, f32[6,128,128]{2,1,0:T(8,128)S(1)}) fusion(bf16[6,512,128]{2,1,0:T(8,128)(2,1)} %bases_ref.1, bf16[512,128]{1,0:T(8,128)(2,1)} %param.3), kind=kOutput, calls=%fused_computation.3 | convolution fusion | flops 100859896 | bytes 1310744 | tf_op jit(solution)/shard_map/qip,iw->qpw/dot_general | solution.py:126
  1.6 0.1 compare_select_fusion
  1.7 0.1 copy_bitcast_fusion
  1.9 0.8 %pad_maximum_fusion = f16[16,56,128]{2,1,0:T(8,128)(2,1)} fusion(f16[16,48,128]{2,1,0:T(8,128)(2,1)S(1)} %copy_bitcast_fusion, f16[56]{0:T(256)(128)(2,1)S(1)} %compare_select_fusion), kind=kLoop, calls=%fused_computation.5 | loop fusion | flops 114688 | bytes 426096 | tf_op jit(solution)/shard_map/concatenate | solution.py:137
  2.7 11.0 %all-to-all-start = ((f16[16,56,128]{2,1,0:T(8,128)(2,1)}), f16[16,56,128]{2,1,0:T(8,128)(2,1)S(1)}, u32[]{:S(2)}, u32[]{:S(2)}) async-start(f16[16,56,128]{2,1,0:T(8,128)(2,1)} %pad_maximum_fusion), calls=%async_computation | async-start | bytes 458752 | tf_op jit(solution)/shard_map/all_to_all | solution.py:140
  13.7 2.3 %collective-permute-start = (bf16[512,128]{1,0:T(8,128)(2,1)}, bf16[512,128]{1,0:T(8,128)(2,1)S(1)}, u32[]{:S(2)}, u32[]{:S(2)}) collective-permute-start(bf16[512,128]{1,0:T(8,128)(2,1)} %param.3), channel_id=1, source_target_pairs={{0,1},{1,0},{2,3},{3,2},{4,5},{5,4},{6,7},{7,6},{8,9},{9,8},{10,11... | collective-permute-start | bytes 393224 | tf_op jit(solution)/shard_map/ppermute | solution.py:150
  16.0 1.2 %collective-permute-done = bf16[512,128]{1,0:T(8,128)(2,1)S(1)} collective-permute-done((bf16[512,128]{1,0:T(8,128)(2,1)}, bf16[512,128]{1,0:T(8,128)(2,1)S(1)}, u32[]{:S(2)}, u32[]{:S(2)}) %collective-permute-start) | collective-permute-done | bytes 131104 | tf_op jit(solution)/shard_map/ppermute | solution.py:150
  17.2 1.0 %maximum_select_fusion.own_ref = bf16[1024,128]{1,0:T(8,128)(2,1)S(1)} fusion(bf16[512,128]{1,0:T(8,128)(2,1)S(1)} %collective-permute-done, bf16[512,128]{1,0:T(8,128)(2,1)} %param.3, pred[]{:T(512)S(6)} %eq.5), kind=kLoop, calls=%fused_computation.4 | loop fusion | flops 1179648 | bytes 524289 | tf_op jit(solution)/shard_map/jit(_where)/select_n | solution.py:151
  18.2 1.2 %all-to-all-done = f16[16,56,128]{2,1,0:T(8,128)(2,1)S(1)} async-done(((f16[16,56,128]{2,1,0:T(8,128)(2,1)}), f16[16,56,128]{2,1,0:T(8,128)(2,1)S(1)}, u32[]{:S(2)}, u32[]{:S(2)}) %all-to-all-start) | async-done | bytes 229408 | tf_op jit(solution)/shard_map/all_to_all | solution.py:140
  19.5 0.0 copy-start.1
  19.5 0.7 %send_far.1 = (f32[32,8,128]{2,1,0:T(8,128)}, f32[2,8,128]{2,1,0:T(8,128)S(1)}) custom-call(f32[16,6,8,128]{3,2,1,0:T(8,128)S(1)} %fusion.incoming_ref), custom_call_target="tpu_custom_call" | custom-call | bytes 393216 | tf_op jit(solution)/shard_map/send_far/pallas_call | solution.py:17
  20.2 14.0 %all-to-all-start.1 = ((f32[32,8,128]{2,1,0:T(8,128)}), f32[32,8,128]{2,1,0:T(8,128)S(1)}, u32[]{:S(2)}, u32[]{:S(2)}) async-start(f32[32,8,128]{2,1,0:T(8,128)} %get-tuple-element.14), calls=%async_computation.1 | async-start | bytes 262144 | tf_op jit(solution)/shard_map/all_to_all | solution.py:160
  34.2 3.3 %collective-permute-start.1 = (bf16[1024,128]{1,0:T(8,128)(2,1)S(1)}, bf16[1024,128]{1,0:T(8,128)(2,1)S(1)}, u32[]{:S(2)}, u32[]{:S(2)}) collective-permute-start(bf16[1024,128]{1,0:T(8,128)(2,1)S(1)} %maximum_select_fusion.own_ref), channel_id=1, source_target_pairs={{0,4},{1,5},{2,6},{3,7},{4,0},{5,1},{6,2},{7,3},{8,12},{9,13},{10,... | collective-permute-start | bytes 786440 | tf_op jit(solution)/shard_map/ppermute | solution.py:163
  37.5 2.5 %collective-permute-start.2 = (bf16[1024,128]{1,0:T(8,128)(2,1)S(1)}, bf16[1024,128]{1,0:T(8,128)(2,1)S(1)}, u32[]{:S(2)}, u32[]{:S(2)}) collective-permute-start(bf16[1024,128]{1,0:T(8,128)(2,1)S(1)} %maximum_select_fusion.own_ref), channel_id=1, source_target_pairs={{0,6},{1,3},{2,0},{3,5},{4,2},{5,7},{6,4},{7,1},{8,14},{9,11},{10,... | collective-permute-start | bytes 786440 | tf_op jit(solution)/shard_map/ppermute | solution.py:163
  39.9 0.2 all-to-all-done.1.far_ref
  40.1 0.7 %gather_siblings.1 = bf16[16,48,128]{2,1,0:T(8,128)(2,1)} custom-call(f32[32,8,128]{2,1,0:T(8,128)S(1)} %all-to-all-done.1.far_ref, f32[2,8,128]{2,1,0:T(8,128)S(1)} %get-tuple-element.15.near_ref), custom_call_target="tpu_custom_call" | custom-call | bytes 139264 | tf_op jit(solution)/shard_map/gather_siblings/pallas_call | solution.py:17
  40.8 6.0 %all-to-all-start.2 = ((bf16[16,48,128]{2,1,0:T(8,128)(2,1)}), bf16[16,48,128]{2,1,0:T(8,128)(2,1)S(1)}, u32[]{:S(2)}, u32[]{:S(2)}) async-start(bf16[16,48,128]{2,1,0:T(8,128)(2,1)} %gather_siblings.1), calls=%async_computation.2 | async-start | bytes 393216 | tf_op jit(solution)/shard_map/all_to_all | solution.py:175
  46.8 2.0 %collective-permute-done.2.side_ref = bf16[1024,128]{1,0:T(8,128)(2,1)S(1)} collective-permute-done((bf16[1024,128]{1,0:T(8,128)(2,1)S(1)}, bf16[1024,128]{1,0:T(8,128)(2,1)S(1)}, u32[]{:S(2)}, u32[]{:S(2)}) %collective-permute-start.2) | collective-permute-done | bytes 262176 | tf_op jit(solution)/shard_map/ppermute | solution.py:163
  48.8 1.9 %collective-permute-start.3 = (bf16[1024,128]{1,0:T(8,128)(2,1)S(1)}, bf16[1024,128]{1,0:T(8,128)(2,1)S(1)}, u32[]{:S(2)}, u32[]{:S(2)}) collective-permute-start(bf16[1024,128]{1,0:T(8,128)(2,1)S(1)} %collective-permute-done.2.side_ref), channel_id=1, source_target_pairs={{0,1},{1,0},{2,3},{3,2},{4,5},{5,4},{6,7},{7,6},{8,9},{9,8},{10,11... | collective-permute-start | bytes 786440 | tf_op jit(solution)/shard_map/ppermute | solution.py:178
  50.7 0.0 copy-start
  50.7 2.2 %copy-done = bf16[512,4096]{1,0:T(8,128)(2,1)S(1)} copy-done((bf16[512,4096]{1,0:T(8,128)(2,1)S(1)}, bf16[512,4096]{1,0:T(8,128)(2,1)}, u32[]{:S(2)}) %copy-start) | copy-done | bytes 4194328
  52.9 1.0 %early_blocks.1 = (f32[512,128]{1,0:T(8,128)S(1)}, bf16[512,1024]{1,0:T(8,128)(2,1)S(1)}) custom-call(bf16[512,4096]{1,0:T(8,128)(2,1)S(1)} %copy-done, bf16[1024,128]{1,0:T(8,128)(2,1)S(1)} %maximum_select_fusion.own_ref, bf16[1024,128]{1,0:T(8,128)(2,1)S(1)} %collective-permute-done.2.side_ref, bf16[1024,128]{1,0:T(8,128)(2,1)S(1)} %collective-permute-done.1.opposite_ref), custom_call_target="tpu_custom_call" | custom-call | bytes 4980736 | tf_op jit(solution)/shard_map/early_blocks/pallas_call | solution.py:17
  54.0 0.4 last_block.1.diagonal_ref
  54.4 1.1 %finish.1 = f32[512,128]{1,0:T(8,128)} custom-call(bf16[6,512,128]{2,1,0:T(8,128)(2,1)S(1)} %copy-done.1, bf16[16,48,128]{2,1,0:T(8,128)(2,1)S(1)} %all-to-all-done.2.spread_ref, f32[512,128]{1,0:T(8,128)S(1)} %last_block.1.diagonal_ref), custom_call_target="tpu_custom_call" | custom-call | flops 50331648 | bytes 1446510 | tf_op jit(solution)/shard_map/finish/pallas_call | solution.py:17
  (8 shorter events, 0.1 us)
Async XLA Ops:
  2.7 16.7 %all-to-all-start = ((f16[16,56,128]{2,1,0:T(8,128)(2,1)}), f16[16,56,128]{2,1,0:T(8,128)(2,1)S(1)}, u32[]{:S(2)}, u32[]{:S(2)}) async-start(f16[16,56,128]{2,1,0:T(8,128)(2,1)} %pad_maximum_fusion), calls=%async_computation | async-start | bytes 458752 | tf_op jit(solution)/shard_map/all_to_all | solution.py:140
  13.7 3.4 %collective-permute-start = (bf16[512,128]{1,0:T(8,128)(2,1)}, bf16[512,128]{1,0:T(8,128)(2,1)S(1)}, u32[]{:S(2)}, u32[]{:S(2)}) collective-permute-start(bf16[512,128]{1,0:T(8,128)(2,1)} %param.3), channel_id=1, source_target_pairs={{0,1},{1,0},{2,3},{3,2},{4,5},{5,4},{6,7},{7,6},{8,9},{9,8},{10,11... | collective-permute-start | bytes 393224 | tf_op jit(solution)/shard_map/ppermute | solution.py:150
  19.5 34.9 %copy-start.1 = (bf16[6,512,128]{2,1,0:T(8,128)(2,1)S(1)}, bf16[6,512,128]{2,1,0:T(8,128)(2,1)}, u32[]{:S(2)}) copy-start(bf16[6,512,128]{2,1,0:T(8,128)(2,1)} %bases_ref.1) | copy-start | bytes 2359300
  20.2 19.9 %all-to-all-start.1 = ((f32[32,8,128]{2,1,0:T(8,128)}), f32[32,8,128]{2,1,0:T(8,128)S(1)}, u32[]{:S(2)}, u32[]{:S(2)}) async-start(f32[32,8,128]{2,1,0:T(8,128)} %get-tuple-element.14), calls=%async_computation.1 | async-start | bytes 262144 | tf_op jit(solution)/shard_map/all_to_all | solution.py:160
  34.2 12.7 %collective-permute-start.1 = (bf16[1024,128]{1,0:T(8,128)(2,1)S(1)}, bf16[1024,128]{1,0:T(8,128)(2,1)S(1)}, u32[]{:S(2)}, u32[]{:S(2)}) collective-permute-start(bf16[1024,128]{1,0:T(8,128)(2,1)S(1)} %maximum_select_fusion.own_ref), channel_id=1, source_target_pairs={{0,4},{1,5},{2,6},{3,7},{4,0},{5,1},{6,2},{7,3},{8,12},{9,13},{10,... | collective-permute-start | bytes 786440 | tf_op jit(solution)/shard_map/ppermute | solution.py:163
  37.5 11.4 %collective-permute-start.2 = (bf16[1024,128]{1,0:T(8,128)(2,1)S(1)}, bf16[1024,128]{1,0:T(8,128)(2,1)S(1)}, u32[]{:S(2)}, u32[]{:S(2)}) collective-permute-start(bf16[1024,128]{1,0:T(8,128)(2,1)S(1)} %maximum_select_fusion.own_ref), channel_id=1, source_target_pairs={{0,6},{1,3},{2,0},{3,5},{4,2},{5,7},{6,4},{7,1},{8,14},{9,11},{10,... | collective-permute-start | bytes 786440 | tf_op jit(solution)/shard_map/ppermute | solution.py:163
  40.8 13.6 %all-to-all-start.2 = ((bf16[16,48,128]{2,1,0:T(8,128)(2,1)}), bf16[16,48,128]{2,1,0:T(8,128)(2,1)S(1)}, u32[]{:S(2)}, u32[]{:S(2)}) async-start(bf16[16,48,128]{2,1,0:T(8,128)(2,1)} %gather_siblings.1), calls=%async_computation.2 | async-start | bytes 393216 | tf_op jit(solution)/shard_map/all_to_all | solution.py:175
  48.8 5.1 %collective-permute-start.3 = (bf16[1024,128]{1,0:T(8,128)(2,1)S(1)}, bf16[1024,128]{1,0:T(8,128)(2,1)S(1)}, u32[]{:S(2)}, u32[]{:S(2)}) collective-permute-start(bf16[1024,128]{1,0:T(8,128)(2,1)S(1)} %collective-permute-done.2.side_ref), channel_id=1, source_target_pairs={{0,1},{1,0},{2,3},{3,2},{4,5},{5,4},{6,7},{7,6},{8,9},{9,8},{10,11... | collective-permute-start | bytes 786440 | tf_op jit(solution)/shard_map/ppermute | solution.py:178
  50.7 2.2 %copy-start = (bf16[512,4096]{1,0:T(8,128)(2,1)S(1)}, bf16[512,4096]{1,0:T(8,128)(2,1)}, u32[]{:S(2)}) copy-start(bf16[512,4096]{1,0:T(8,128)(2,1)} %rows_ref.1) | copy-start | bytes 12582916

commit v4 on v3

--- a/solution.py
+++ b/solution.py
@@ -89,15 +89,11 @@
     rest_ref[...] = columns(rows_ref, 2 * (chip + 3 - 2 * core), 2)
 
 
-def last_block(rest_ref, other_ref, early_ref, out_ref):
-    out_ref[...] = early_ref[...] + jnp.dot(
+def finish(rest_ref, other_ref, early_ref, bases_ref, spread_ref, out_ref):
+    level_count = bases_ref.shape[0]
+    total = early_ref[...] + jnp.dot(
         rest_ref[...], other_ref[...], preferred_element_type=jnp.float32
     )
-
-
-def finish(bases_ref, spread_ref, diagonal_ref, out_ref):
-    level_count = bases_ref.shape[0]
-    total = diagonal_ref[...]
     slices = [spread_ref[k].astype(jnp.float32) for k in range(PAIR_DEVS)]
     deep = slices[0].shape[0] // level_count
     for level in range(0, level_count, 2):
@@ -128,14 +124,19 @@
     )
     largest = jnp.max(jnp.abs(partial), axis=(1, 2))
     power = 14.0 - jnp.ceil(jnp.log2(jnp.maximum(largest, 1e-30)))
-    scaled = (partial * jnp.exp2(power)[:, None, None]).astype(jnp.float16)
-    powers = jnp.broadcast_to(
-        jnp.pad(power, (0, slice_rows - level_count))[None, :, None],
-        (PAIR_DEVS, slice_rows, width),
-    ).astype(jnp.float16)
-    outgoing = scaled.reshape(level_count, PAIR_DEVS, slice_rows, width).swapaxes(0, 1)
+    powers = jnp.tile(jnp.pad(power, (0, slice_rows - level_count)), PAIR_DEVS)
     outgoing = jnp.concatenate(
-        [outgoing.reshape(PAIR_DEVS, level_count * slice_rows, width), powers], 1
+        [
+            partial * jnp.exp2(power)[:, None, None],
+            jnp.broadcast_to(powers[None, :, None], (1, rank, width)),
+        ],
+        0,
+    )
+    outgoing = (
+        outgoing.reshape(level_count + 1, PAIR_DEVS, slice_rows, width)
+        .swapaxes(0, 1)
+        .reshape(PAIR_DEVS, (level_count + 1) * slice_rows, width)
+        .astype(jnp.float16)
     )
     received = lax.all_to_all(outgoing, "leaf", 0, 0, axis_index_groups=near)
     received = received.astype(jnp.float32)
@@ -185,8 +186,7 @@
         side,
         opposite,
     )
-    product = call(last_block, f32(points, width), 0, rest, other, early)
-    return call(finish, f32(points, width), bases.size * width, bases, spread, product)
+    return call(finish, f32(points, width), 0, rest, other, early, bases, spread)
 
 
 def solution(mesh):

time: 56 us -> 55.9 us (level)
    concatenate x2 -> x0, other arithmetic: 0.89 us -> none  [shards(): jnp.concatenate([outgoing.reshape(PAIR_DEVS, level_count * slice_rows, wi...]
    convert_element_type x0 -> x1, other arithmetic: none -> 0.75 us  [shards(): outgoing = outgoing.reshape(level_count + 1, PAIR_DEVS, slice_rows, width...]
    pallas_call x5 -> x4, Pallas kernels: 3.93 us -> 3.76 us  [call(): pl.pallas_call(kernel, out_shape=outs, in_specs=[VMEM] * len(args), out_s...]
  transfers between devices with their start and end apart: 7 -> 7, of which waited for: 4 -> 4; matrix products, arithmetic and copies ran while one was open for 2% -> 2% of each run, Pallas kernels for 4% -> 3%
where the time goes in v4:
time: 55.9 us; the launch traced here: 55.4 us
  starting transfers between devices  40.9 us (73%)
  waiting for transfers between devices  4.49 us (8%)
  Pallas kernels  3.76 us (7%)
  local copies, waits for them, and re-layouts  2.38 us (4%)
  other arithmetic  2.02 us (4%)
  matrix products  1.63 us (3%)
    all_to_all x1, starting transfers between devices, shards(): from_far = lax.all_to_all(to_far, 'leaf', 0, 0, axis_index_groups=far)  14 us
    all_to_all x1, starting transfers between devices, shards(): received = lax.all_to_all(outgoing, 'leaf', 0, 0, axis_index_groups=near)  11 us
    all_to_all x1, starting transfers between devices, shards(): spread = lax.all_to_all(spread, 'leaf', 0, 0, axis_index_groups=near)  6.03 us
    ppermute x2, starting transfers between devices, shards(): lax.ppermute(own, 'leaf', [(i, leaf_of(i) + (i + step[i % 2]) % LEAF_DEVS...  5.73 us
    pallas_call x4, Pallas kernels, call(): pl.pallas_call(kernel, out_shape=outs, in_specs=[VMEM] * len(args), out_s...  3.76 us
    ppermute x1, starting transfers between devices, shards(): twin = lax.ppermute(right_side_block, 'leaf', swap)  2.26 us
    unnamed x4, local copies, waits for them, and re-layouts  2.19 us
    ppermute x2, waiting for transfers between devices, shards(): lax.ppermute(own, 'leaf', [(i, leaf_of(i) + (i + step[i % 2]) % LEAF_DEVS...  1.96 us
  transfers between devices with their start and end apart: 7, of which 4 were waited for; matrix products, arithmetic and copies ran while one was open for 2% of the time, Pallas kernels for 3%

profile of v4, /device:TPU:1, one launch (start us, length us, event | category | flops | bytes accessed | tf_op | source)
XLA Modules:
  0.0 55.4 jit_solution(15207294906639046632)
XLA Ops:
  0.0 1.6 %abs_reduce_fusion = (f32[6]{0:T(128)S(1)}, f32[6,128,128]{2,1,0:T(8,128)S(1)}) fusion(bf16[6,512,128]{2,1,0:T(8,128)(2,1)} %bases_ref.1, bf16[512,128]{1,0:T(8,128)(2,1)} %param.3), kind=kOutput, calls=%fused_computation.3 | convolution fusion | flops 100859896 | bytes 1310744 | tf_op jit(solution)/shard_map/qip,iw->qpw/dot_general | solution.py:122
  1.7 0.1 reshape.22
  1.8 0.1 multiply_convert_fusion
  1.9 0.1 broadcast_in_dim.10
  2.0 0.8 %copy_bitcast_fusion = f16[16,56,128]{2,1,0:T(8,128)(2,1)} fusion(f16[1,128,128]{2,1,0:T(8,128)(2,1)S(1)} %broadcast_in_dim.10, f16[6,128,128]{2,1,0:T(8,128)(2,1)S(1)} %multiply_convert_fusion), kind=kLoop, calls=%fused_computation.6 | loop fusion | flops 114688 | bytes 458752 | tf_op jit(solution)/shard_map/convert_element_type | solution.py:139
  2.7 11.0 %all-to-all-start = ((f16[16,56,128]{2,1,0:T(8,128)(2,1)}), f16[16,56,128]{2,1,0:T(8,128)(2,1)S(1)}, u32[]{:S(2)}, u32[]{:S(2)}) async-start(f16[16,56,128]{2,1,0:T(8,128)(2,1)} %copy_bitcast_fusion), calls=%async_computation | async-start | bytes 458752 | tf_op jit(solution)/shard_map/all_to_all | solution.py:141
  13.8 2.3 %collective-permute-start = (bf16[512,128]{1,0:T(8,128)(2,1)}, bf16[512,128]{1,0:T(8,128)(2,1)S(1)}, u32[]{:S(2)}, u32[]{:S(2)}) collective-permute-start(bf16[512,128]{1,0:T(8,128)(2,1)} %param.3), channel_id=1, source_target_pairs={{0,1},{1,0},{2,3},{3,2},{4,5},{5,4},{6,7},{7,6},{8,9},{9,8},{10,11... | collective-permute-start | bytes 393224 | tf_op jit(solution)/shard_map/ppermute | solution.py:151
  16.1 0.0 copy-start.1
  16.1 1.2 %collective-permute-done = bf16[512,128]{1,0:T(8,128)(2,1)S(1)} collective-permute-done((bf16[512,128]{1,0:T(8,128)(2,1)}, bf16[512,128]{1,0:T(8,128)(2,1)S(1)}, u32[]{:S(2)}, u32[]{:S(2)}) %collective-permute-start) | collective-permute-done | bytes 131104 | tf_op jit(solution)/shard_map/ppermute | solution.py:151
  17.2 1.0 %maximum_select_fusion.own_ref = bf16[1024,128]{1,0:T(8,128)(2,1)S(1)} fusion(bf16[512,128]{1,0:T(8,128)(2,1)S(1)} %collective-permute-done, bf16[512,128]{1,0:T(8,128)(2,1)} %param.3, pred[]{:T(512)S(6)} %eq.5), kind=kLoop, calls=%fused_computation.4 | loop fusion | flops 1179648 | bytes 524289 | tf_op jit(solution)/shard_map/jit(_where)/select_n | solution.py:152
  18.3 1.2 %all-to-all-done = f16[16,56,128]{2,1,0:T(8,128)(2,1)S(1)} async-done(((f16[16,56,128]{2,1,0:T(8,128)(2,1)}), f16[16,56,128]{2,1,0:T(8,128)(2,1)S(1)}, u32[]{:S(2)}, u32[]{:S(2)}) %all-to-all-start) | async-done | bytes 229408 | tf_op jit(solution)/shard_map/all_to_all | solution.py:141
  19.6 0.7 %send_far.1 = (f32[32,8,128]{2,1,0:T(8,128)}, f32[2,8,128]{2,1,0:T(8,128)S(1)}) custom-call(f32[16,6,8,128]{3,2,1,0:T(8,128)S(1)} %fusion.incoming_ref), custom_call_target="tpu_custom_call" | custom-call | bytes 393216 | tf_op jit(solution)/shard_map/send_far/pallas_call | solution.py:17
  20.3 14.0 %all-to-all-start.1 = ((f32[32,8,128]{2,1,0:T(8,128)}), f32[32,8,128]{2,1,0:T(8,128)S(1)}, u32[]{:S(2)}, u32[]{:S(2)}) async-start(f32[32,8,128]{2,1,0:T(8,128)} %get-tuple-element.19), calls=%async_computation.1 | async-start | bytes 262144 | tf_op jit(solution)/shard_map/all_to_all | solution.py:161
  34.2 3.3 %collective-permute-start.1 = (bf16[1024,128]{1,0:T(8,128)(2,1)S(1)}, bf16[1024,128]{1,0:T(8,128)(2,1)S(1)}, u32[]{:S(2)}, u32[]{:S(2)}) collective-permute-start(bf16[1024,128]{1,0:T(8,128)(2,1)S(1)} %maximum_select_fusion.own_ref), channel_id=1, source_target_pairs={{0,4},{1,5},{2,6},{3,7},{4,0},{5,1},{6,2},{7,3},{8,12},{9,13},{10,... | collective-permute-start | bytes 786440 | tf_op jit(solution)/shard_map/ppermute | solution.py:164
  37.5 2.5 %collective-permute-start.2 = (bf16[1024,128]{1,0:T(8,128)(2,1)S(1)}, bf16[1024,128]{1,0:T(8,128)(2,1)S(1)}, u32[]{:S(2)}, u32[]{:S(2)}) collective-permute-start(bf16[1024,128]{1,0:T(8,128)(2,1)S(1)} %maximum_select_fusion.own_ref), channel_id=1, source_target_pairs={{0,6},{1,3},{2,0},{3,5},{4,2},{5,7},{6,4},{7,1},{8,14},{9,11},{10,... | collective-permute-start | bytes 786440 | tf_op jit(solution)/shard_map/ppermute | solution.py:164
  40.0 0.2 all-to-all-done.1.far_ref
  40.2 0.7 %gather_siblings.1 = bf16[16,48,128]{2,1,0:T(8,128)(2,1)} custom-call(f32[32,8,128]{2,1,0:T(8,128)S(1)} %all-to-all-done.1.far_ref, f32[2,8,128]{2,1,0:T(8,128)S(1)} %get-tuple-element.20.near_ref), custom_call_target="tpu_custom_call" | custom-call | bytes 139264 | tf_op jit(solution)/shard_map/gather_siblings/pallas_call | solution.py:17
  40.9 6.0 %all-to-all-start.2 = ((bf16[16,48,128]{2,1,0:T(8,128)(2,1)}), bf16[16,48,128]{2,1,0:T(8,128)(2,1)S(1)}, u32[]{:S(2)}, u32[]{:S(2)}) async-start(bf16[16,48,128]{2,1,0:T(8,128)(2,1)} %gather_siblings.1), calls=%async_computation.2 | async-start | bytes 393216 | tf_op jit(solution)/shard_map/all_to_all | solution.py:176
  46.9 2.0 %collective-permute-done.2.side_ref = bf16[1024,128]{1,0:T(8,128)(2,1)S(1)} collective-permute-done((bf16[1024,128]{1,0:T(8,128)(2,1)S(1)}, bf16[1024,128]{1,0:T(8,128)(2,1)S(1)}, u32[]{:S(2)}, u32[]{:S(2)}) %collective-permute-start.2) | collective-permute-done | bytes 262176 | tf_op jit(solution)/shard_map/ppermute | solution.py:164
  48.9 1.9 %collective-permute-start.3 = (bf16[1024,128]{1,0:T(8,128)(2,1)S(1)}, bf16[1024,128]{1,0:T(8,128)(2,1)S(1)}, u32[]{:S(2)}, u32[]{:S(2)}) collective-permute-start(bf16[1024,128]{1,0:T(8,128)(2,1)S(1)} %collective-permute-done.2.side_ref), channel_id=1, source_target_pairs={{0,1},{1,0},{2,3},{3,2},{4,5},{5,4},{6,7},{7,6},{8,9},{9,8},{10,11... | collective-permute-start | bytes 786440 | tf_op jit(solution)/shard_map/ppermute | solution.py:179
  50.8 0.0 copy-start
  50.8 2.2 %copy-done = bf16[512,4096]{1,0:T(8,128)(2,1)S(1)} copy-done((bf16[512,4096]{1,0:T(8,128)(2,1)S(1)}, bf16[512,4096]{1,0:T(8,128)(2,1)}, u32[]{:S(2)}) %copy-start) | copy-done | bytes 4194328
  53.0 1.0 %early_blocks.1 = (f32[512,128]{1,0:T(8,128)S(1)}, bf16[512,1024]{1,0:T(8,128)(2,1)S(1)}) custom-call(bf16[512,4096]{1,0:T(8,128)(2,1)S(1)} %copy-done, bf16[1024,128]{1,0:T(8,128)(2,1)S(1)} %maximum_select_fusion.own_ref, bf16[1024,128]{1,0:T(8,128)(2,1)S(1)} %collective-permute-done.2.side_ref, bf16[1024,128]{1,0:T(8,128)(2,1)S(1)} %collective-permute-done.1.opposite_ref), custom_call_target="tpu_custom_call" | custom-call | bytes 4980736 | tf_op jit(solution)/shard_map/early_blocks/pallas_call | solution.py:17
  54.0 1.3 %finish.1 = f32[512,128]{1,0:T(8,128)} custom-call(bf16[512,1024]{1,0:T(8,128)(2,1)S(1)} %get-tuple-element.17.rest_ref, bf16[1024,128]{1,0:T(8,128)(2,1)S(1)} %collective-permute-done.3.other_ref, f32[512,128]{1,0:T(8,128)S(1)} %get-tuple-element.18.early_ref, bf16[6,512,128]{2,1,0:T(8,128)(2,1)S(1)} %copy-done.1, ...), custom_call_target="tpu_custom_call" | custom-call | bytes 2555904 | tf_op jit(solution)/shard_map/finish/pallas_call | solution.py:17
  (10 shorter events, 0.1 us)
Async XLA Ops:
  2.7 16.7 %all-to-all-start = ((f16[16,56,128]{2,1,0:T(8,128)(2,1)}), f16[16,56,128]{2,1,0:T(8,128)(2,1)S(1)}, u32[]{:S(2)}, u32[]{:S(2)}) async-start(f16[16,56,128]{2,1,0:T(8,128)(2,1)} %copy_bitcast_fusion), calls=%async_computation | async-start | bytes 458752 | tf_op jit(solution)/shard_map/all_to_all | solution.py:141
  13.8 3.4 %collective-permute-start = (bf16[512,128]{1,0:T(8,128)(2,1)}, bf16[512,128]{1,0:T(8,128)(2,1)S(1)}, u32[]{:S(2)}, u32[]{:S(2)}) collective-permute-start(bf16[512,128]{1,0:T(8,128)(2,1)} %param.3), channel_id=1, source_target_pairs={{0,1},{1,0},{2,3},{3,2},{4,5},{5,4},{6,7},{7,6},{8,9},{9,8},{10,11... | collective-permute-start | bytes 393224 | tf_op jit(solution)/shard_map/ppermute | solution.py:151
  16.1 38.0 %copy-start.1 = (bf16[6,512,128]{2,1,0:T(8,128)(2,1)S(1)}, bf16[6,512,128]{2,1,0:T(8,128)(2,1)}, u32[]{:S(2)}) copy-start(bf16[6,512,128]{2,1,0:T(8,128)(2,1)} %bases_ref.1) | copy-start | bytes 2359300
  20.3 19.9 %all-to-all-start.1 = ((f32[32,8,128]{2,1,0:T(8,128)}), f32[32,8,128]{2,1,0:T(8,128)S(1)}, u32[]{:S(2)}, u32[]{:S(2)}) async-start(f32[32,8,128]{2,1,0:T(8,128)} %get-tuple-element.19), calls=%async_computation.1 | async-start | bytes 262144 | tf_op jit(solution)/shard_map/all_to_all | solution.py:161
  34.2 12.7 %collective-permute-start.1 = (bf16[1024,128]{1,0:T(8,128)(2,1)S(1)}, bf16[1024,128]{1,0:T(8,128)(2,1)S(1)}, u32[]{:S(2)}, u32[]{:S(2)}) collective-permute-start(bf16[1024,128]{1,0:T(8,128)(2,1)S(1)} %maximum_select_fusion.own_ref), channel_id=1, source_target_pairs={{0,4},{1,5},{2,6},{3,7},{4,0},{5,1},{6,2},{7,3},{8,12},{9,13},{10,... | collective-permute-start | bytes 786440 | tf_op jit(solution)/shard_map/ppermute | solution.py:164
  37.5 11.4 %collective-permute-start.2 = (bf16[1024,128]{1,0:T(8,128)(2,1)S(1)}, bf16[1024,128]{1,0:T(8,128)(2,1)S(1)}, u32[]{:S(2)}, u32[]{:S(2)}) collective-permute-start(bf16[1024,128]{1,0:T(8,128)(2,1)S(1)} %maximum_select_fusion.own_ref), channel_id=1, source_target_pairs={{0,6},{1,3},{2,0},{3,5},{4,2},{5,7},{6,4},{7,1},{8,14},{9,11},{10,... | collective-permute-start | bytes 786440 | tf_op jit(solution)/shard_map/ppermute | solution.py:164
  40.9 13.1 %all-to-all-start.2 = ((bf16[16,48,128]{2,1,0:T(8,128)(2,1)}), bf16[16,48,128]{2,1,0:T(8,128)(2,1)S(1)}, u32[]{:S(2)}, u32[]{:S(2)}) async-start(bf16[16,48,128]{2,1,0:T(8,128)(2,1)} %gather_siblings.1), calls=%async_computation.2 | async-start | bytes 393216 | tf_op jit(solution)/shard_map/all_to_all | solution.py:176
  48.9 5.1 %collective-permute-start.3 = (bf16[1024,128]{1,0:T(8,128)(2,1)S(1)}, bf16[1024,128]{1,0:T(8,128)(2,1)S(1)}, u32[]{:S(2)}, u32[]{:S(2)}) collective-permute-start(bf16[1024,128]{1,0:T(8,128)(2,1)S(1)} %collective-permute-done.2.side_ref), channel_id=1, source_target_pairs={{0,1},{1,0},{2,3},{3,2},{4,5},{5,4},{6,7},{7,6},{8,9},{9,8},{10,11... | collective-permute-start | bytes 786440 | tf_op jit(solution)/shard_map/ppermute | solution.py:179
  50.8 2.2 %copy-start = (bf16[512,4096]{1,0:T(8,128)(2,1)S(1)}, bf16[512,4096]{1,0:T(8,128)(2,1)}, u32[]{:S(2)}) copy-start(bf16[512,4096]{1,0:T(8,128)(2,1)} %rows_ref.1) | copy-start | bytes 12582916

commit v5 on v4

--- a/solution.py
+++ b/solution.py
@@ -8,7 +8,7 @@
 CHIPS = 4
 LEAF_DEVS = 2 * CHIPS
 PAIR_DEVS = 2 * LEAF_DEVS
-LATE_PAIR = 30
+LATE_PAIR = 22
 LATE_PLACE = 6
 VMEM = pl.BlockSpec(memory_space=pltpu.VMEM)
 

time: 55.9 us -> 55.6 us (level)
  waiting for transfers between devices: 4.49 us -> 3.65 us
    ppermute x2, waiting for transfers between devices: 1.96 us -> 1.29 us  [shards(): lax.ppermute(own, 'leaf', [(i, leaf_of(i) + (i + step[i % 2]) % LEAF_DEVS...]
  transfers between devices with their start and end apart: 7 -> 7, of which waited for: 4 -> 3; matrix products, arithmetic and copies ran while one was open for 2% -> 2% of each run, Pallas kernels for 3% -> 3%
where the time goes in v5:
time: 55.6 us; the launch traced here: 55.1 us
  starting transfers between devices  41.4 us (74%)
  Pallas kernels  3.77 us (7%)
  waiting for transfers between devices  3.65 us (7%)
  local copies, waits for them, and re-layouts  2.38 us (4%)
  other arithmetic  2.02 us (4%)
  matrix products  1.63 us (3%)
    all_to_all x1, starting transfers between devices, shards(): from_far = lax.all_to_all(to_far, 'leaf', 0, 0, axis_index_groups=far)  14 us
    all_to_all x1, starting transfers between devices, shards(): received = lax.all_to_all(outgoing, 'leaf', 0, 0, axis_index_groups=near)  11 us
    all_to_all x1, starting transfers between devices, shards(): spread = lax.all_to_all(spread, 'leaf', 0, 0, axis_index_groups=near)  6.47 us
    ppermute x2, starting transfers between devices, shards(): lax.ppermute(own, 'leaf', [(i, leaf_of(i) + (i + step[i % 2]) % LEAF_DEVS...  5.73 us
    pallas_call x4, Pallas kernels, call(): pl.pallas_call(kernel, out_shape=outs, in_specs=[VMEM] * len(args), out_s...  3.77 us
    ppermute x1, starting transfers between devices, shards(): twin = lax.ppermute(right_side_block, 'leaf', swap)  2.26 us
    unnamed x4, local copies, waits for them, and re-layouts  2.19 us
    ppermute x1, starting transfers between devices, shards(): other = lax.ppermute(side, 'leaf', swap)  1.91 us
  transfers between devices with their start and end apart: 7, of which 3 were waited for; matrix products, arithmetic and copies ran while one was open for 2% of the time, Pallas kernels for 3%

profile of v5, /device:TPU:1, one launch (start us, length us, event | category | flops | bytes accessed | tf_op | source)
XLA Modules:
  0.0 55.1 jit_solution(13720939519249268527)
XLA Ops:
  0.0 1.6 %abs_reduce_fusion = (f32[6]{0:T(128)S(1)}, f32[6,128,128]{2,1,0:T(8,128)S(1)}) fusion(bf16[6,512,128]{2,1,0:T(8,128)(2,1)} %bases_ref.1, bf16[512,128]{1,0:T(8,128)(2,1)} %param.3), kind=kOutput, calls=%fused_computation.3 | convolution fusion | flops 100859896 | bytes 1310744 | tf_op jit(solution)/shard_map/qip,iw->qpw/dot_general | solution.py:122
  1.7 0.1 reshape.22
  1.8 0.1 multiply_convert_fusion
  1.9 0.1 broadcast_in_dim.10
  2.0 0.8 %copy_bitcast_fusion = f16[16,56,128]{2,1,0:T(8,128)(2,1)} fusion(f16[1,128,128]{2,1,0:T(8,128)(2,1)S(1)} %broadcast_in_dim.10, f16[6,128,128]{2,1,0:T(8,128)(2,1)S(1)} %multiply_convert_fusion), kind=kLoop, calls=%fused_computation.6 | loop fusion | flops 114688 | bytes 458752 | tf_op jit(solution)/shard_map/convert_element_type | solution.py:139
  2.7 11.0 %all-to-all-start = ((f16[16,56,128]{2,1,0:T(8,128)(2,1)}), f16[16,56,128]{2,1,0:T(8,128)(2,1)S(1)}, u32[]{:S(2)}, u32[]{:S(2)}) async-start(f16[16,56,128]{2,1,0:T(8,128)(2,1)} %copy_bitcast_fusion), calls=%async_computation | async-start | bytes 458752 | tf_op jit(solution)/shard_map/all_to_all | solution.py:141
  13.8 2.3 %collective-permute-start = (bf16[512,128]{1,0:T(8,128)(2,1)}, bf16[512,128]{1,0:T(8,128)(2,1)S(1)}, u32[]{:S(2)}, u32[]{:S(2)}) collective-permute-start(bf16[512,128]{1,0:T(8,128)(2,1)} %param.3), channel_id=1, source_target_pairs={{0,1},{1,0},{2,3},{3,2},{4,5},{5,4},{6,7},{7,6},{8,9},{9,8},{10,11... | collective-permute-start | bytes 393224 | tf_op jit(solution)/shard_map/ppermute | solution.py:151
  16.1 0.0 copy-start.1
  16.1 1.2 %collective-permute-done = bf16[512,128]{1,0:T(8,128)(2,1)S(1)} collective-permute-done((bf16[512,128]{1,0:T(8,128)(2,1)}, bf16[512,128]{1,0:T(8,128)(2,1)S(1)}, u32[]{:S(2)}, u32[]{:S(2)}) %collective-permute-start) | collective-permute-done | bytes 131104 | tf_op jit(solution)/shard_map/ppermute | solution.py:151
  17.2 1.0 %maximum_select_fusion.own_ref = bf16[1024,128]{1,0:T(8,128)(2,1)S(1)} fusion(bf16[512,128]{1,0:T(8,128)(2,1)S(1)} %collective-permute-done, bf16[512,128]{1,0:T(8,128)(2,1)} %param.3, pred[]{:T(512)S(6)} %eq.5), kind=kLoop, calls=%fused_computation.4 | loop fusion | flops 1179648 | bytes 524289 | tf_op jit(solution)/shard_map/jit(_where)/select_n | solution.py:152
  18.3 1.2 %all-to-all-done = f16[16,56,128]{2,1,0:T(8,128)(2,1)S(1)} async-done(((f16[16,56,128]{2,1,0:T(8,128)(2,1)}), f16[16,56,128]{2,1,0:T(8,128)(2,1)S(1)}, u32[]{:S(2)}, u32[]{:S(2)}) %all-to-all-start) | async-done | bytes 229408 | tf_op jit(solution)/shard_map/all_to_all | solution.py:141
  19.6 0.7 %send_far.1 = (f32[32,8,128]{2,1,0:T(8,128)}, f32[2,8,128]{2,1,0:T(8,128)S(1)}) custom-call(f32[16,6,8,128]{3,2,1,0:T(8,128)S(1)} %fusion.incoming_ref), custom_call_target="tpu_custom_call" | custom-call | bytes 393216 | tf_op jit(solution)/shard_map/send_far/pallas_call | solution.py:17
  20.3 14.0 %all-to-all-start.1 = ((f32[32,8,128]{2,1,0:T(8,128)}), f32[32,8,128]{2,1,0:T(8,128)S(1)}, u32[]{:S(2)}, u32[]{:S(2)}) async-start(f32[32,8,128]{2,1,0:T(8,128)} %get-tuple-element.19), calls=%async_computation.1 | async-start | bytes 262144 | tf_op jit(solution)/shard_map/all_to_all | solution.py:161
  34.3 3.3 %collective-permute-start.1 = (bf16[1024,128]{1,0:T(8,128)(2,1)S(1)}, bf16[1024,128]{1,0:T(8,128)(2,1)S(1)}, u32[]{:S(2)}, u32[]{:S(2)}) collective-permute-start(bf16[1024,128]{1,0:T(8,128)(2,1)S(1)} %maximum_select_fusion.own_ref), channel_id=1, source_target_pairs={{0,4},{1,5},{2,6},{3,7},{4,0},{5,1},{6,2},{7,3},{8,12},{9,13},{10,... | collective-permute-start | bytes 786440 | tf_op jit(solution)/shard_map/ppermute | solution.py:164
  37.6 2.5 %collective-permute-start.2 = (bf16[1024,128]{1,0:T(8,128)(2,1)S(1)}, bf16[1024,128]{1,0:T(8,128)(2,1)S(1)}, u32[]{:S(2)}, u32[]{:S(2)}) collective-permute-start(bf16[1024,128]{1,0:T(8,128)(2,1)S(1)} %maximum_select_fusion.own_ref), channel_id=1, source_target_pairs={{0,6},{1,3},{2,0},{3,5},{4,2},{5,7},{6,4},{7,1},{8,14},{9,11},{10,... | collective-permute-start | bytes 786440 | tf_op jit(solution)/shard_map/ppermute | solution.py:164
  40.1 0.0 all-to-all-done.1.far_ref
  40.1 0.7 %gather_siblings.1 = bf16[16,48,128]{2,1,0:T(8,128)(2,1)} custom-call(f32[32,8,128]{2,1,0:T(8,128)S(1)} %all-to-all-done.1.far_ref, f32[2,8,128]{2,1,0:T(8,128)S(1)} %get-tuple-element.20.near_ref), custom_call_target="tpu_custom_call" | custom-call | bytes 139264 | tf_op jit(solution)/shard_map/gather_siblings/pallas_call | solution.py:17
  40.8 6.5 %all-to-all-start.2 = ((bf16[16,48,128]{2,1,0:T(8,128)(2,1)}), bf16[16,48,128]{2,1,0:T(8,128)(2,1)S(1)}, u32[]{:S(2)}, u32[]{:S(2)}) async-start(bf16[16,48,128]{2,1,0:T(8,128)(2,1)} %gather_siblings.1), calls=%async_computation.2 | async-start | bytes 393216 | tf_op jit(solution)/shard_map/all_to_all | solution.py:176
  47.2 1.3 %collective-permute-done.2.side_ref = bf16[1024,128]{1,0:T(8,128)(2,1)S(1)} collective-permute-done((bf16[1024,128]{1,0:T(8,128)(2,1)S(1)}, bf16[1024,128]{1,0:T(8,128)(2,1)S(1)}, u32[]{:S(2)}, u32[]{:S(2)}) %collective-permute-start.2) | collective-permute-done | bytes 262176 | tf_op jit(solution)/shard_map/ppermute | solution.py:164
  48.5 1.9 %collective-permute-start.3 = (bf16[1024,128]{1,0:T(8,128)(2,1)S(1)}, bf16[1024,128]{1,0:T(8,128)(2,1)S(1)}, u32[]{:S(2)}, u32[]{:S(2)}) collective-permute-start(bf16[1024,128]{1,0:T(8,128)(2,1)S(1)} %collective-permute-done.2.side_ref), channel_id=1, source_target_pairs={{0,1},{1,0},{2,3},{3,2},{4,5},{5,4},{6,7},{7,6},{8,9},{9,8},{10,11... | collective-permute-start | bytes 786440 | tf_op jit(solution)/shard_map/ppermute | solution.py:179
  50.5 0.0 copy-start
  50.5 2.2 %copy-done = bf16[512,4096]{1,0:T(8,128)(2,1)S(1)} copy-done((bf16[512,4096]{1,0:T(8,128)(2,1)S(1)}, bf16[512,4096]{1,0:T(8,128)(2,1)}, u32[]{:S(2)}) %copy-start) | copy-done | bytes 4194328
  52.6 1.0 %early_blocks.1 = (f32[512,128]{1,0:T(8,128)S(1)}, bf16[512,1024]{1,0:T(8,128)(2,1)S(1)}) custom-call(bf16[512,4096]{1,0:T(8,128)(2,1)S(1)} %copy-done, bf16[1024,128]{1,0:T(8,128)(2,1)S(1)} %maximum_select_fusion.own_ref, bf16[1024,128]{1,0:T(8,128)(2,1)S(1)} %collective-permute-done.2.side_ref, bf16[1024,128]{1,0:T(8,128)(2,1)S(1)} %collective-permute-done.1.opposite_ref), custom_call_target="tpu_custom_call" | custom-call | bytes 4980736 | tf_op jit(solution)/shard_map/early_blocks/pallas_call | solution.py:17
  53.7 1.3 %finish.1 = f32[512,128]{1,0:T(8,128)} custom-call(bf16[512,1024]{1,0:T(8,128)(2,1)S(1)} %get-tuple-element.17.rest_ref, bf16[1024,128]{1,0:T(8,128)(2,1)S(1)} %collective-permute-done.3.other_ref, f32[512,128]{1,0:T(8,128)S(1)} %get-tuple-element.18.early_ref, bf16[6,512,128]{2,1,0:T(8,128)(2,1)S(1)} %copy-done.1, ...), custom_call_target="tpu_custom_call" | custom-call | bytes 2555904 | tf_op jit(solution)/shard_map/finish/pallas_call | solution.py:17
  (10 shorter events, 0.1 us)
Async XLA Ops:
  2.7 16.7 %all-to-all-start = ((f16[16,56,128]{2,1,0:T(8,128)(2,1)}), f16[16,56,128]{2,1,0:T(8,128)(2,1)S(1)}, u32[]{:S(2)}, u32[]{:S(2)}) async-start(f16[16,56,128]{2,1,0:T(8,128)(2,1)} %copy_bitcast_fusion), calls=%async_computation | async-start | bytes 458752 | tf_op jit(solution)/shard_map/all_to_all | solution.py:141
  13.8 3.4 %collective-permute-start = (bf16[512,128]{1,0:T(8,128)(2,1)}, bf16[512,128]{1,0:T(8,128)(2,1)S(1)}, u32[]{:S(2)}, u32[]{:S(2)}) collective-permute-start(bf16[512,128]{1,0:T(8,128)(2,1)} %param.3), channel_id=1, source_target_pairs={{0,1},{1,0},{2,3},{3,2},{4,5},{5,4},{6,7},{7,6},{8,9},{9,8},{10,11... | collective-permute-start | bytes 393224 | tf_op jit(solution)/shard_map/ppermute | solution.py:151
  16.1 37.6 %copy-start.1 = (bf16[6,512,128]{2,1,0:T(8,128)(2,1)S(1)}, bf16[6,512,128]{2,1,0:T(8,128)(2,1)}, u32[]{:S(2)}) copy-start(bf16[6,512,128]{2,1,0:T(8,128)(2,1)} %bases_ref.1) | copy-start | bytes 2359300
  20.3 19.8 %all-to-all-start.1 = ((f32[32,8,128]{2,1,0:T(8,128)}), f32[32,8,128]{2,1,0:T(8,128)S(1)}, u32[]{:S(2)}, u32[]{:S(2)}) async-start(f32[32,8,128]{2,1,0:T(8,128)} %get-tuple-element.19), calls=%async_computation.1 | async-start | bytes 262144 | tf_op jit(solution)/shard_map/all_to_all | solution.py:161
  34.3 12.9 %collective-permute-start.1 = (bf16[1024,128]{1,0:T(8,128)(2,1)S(1)}, bf16[1024,128]{1,0:T(8,128)(2,1)S(1)}, u32[]{:S(2)}, u32[]{:S(2)}) collective-permute-start(bf16[1024,128]{1,0:T(8,128)(2,1)S(1)} %maximum_select_fusion.own_ref), channel_id=1, source_target_pairs={{0,4},{1,5},{2,6},{3,7},{4,0},{5,1},{6,2},{7,3},{8,12},{9,13},{10,... | collective-permute-start | bytes 786440 | tf_op jit(solution)/shard_map/ppermute | solution.py:164
  37.6 11.0 %collective-permute-start.2 = (bf16[1024,128]{1,0:T(8,128)(2,1)S(1)}, bf16[1024,128]{1,0:T(8,128)(2,1)S(1)}, u32[]{:S(2)}, u32[]{:S(2)}) collective-permute-start(bf16[1024,128]{1,0:T(8,128)(2,1)S(1)} %maximum_select_fusion.own_ref), channel_id=1, source_target_pairs={{0,6},{1,3},{2,0},{3,5},{4,2},{5,7},{6,4},{7,1},{8,14},{9,11},{10,... | collective-permute-start | bytes 786440 | tf_op jit(solution)/shard_map/ppermute | solution.py:164
  40.8 12.9 %all-to-all-start.2 = ((bf16[16,48,128]{2,1,0:T(8,128)(2,1)}), bf16[16,48,128]{2,1,0:T(8,128)(2,1)S(1)}, u32[]{:S(2)}, u32[]{:S(2)}) async-start(bf16[16,48,128]{2,1,0:T(8,128)(2,1)} %gather_siblings.1), calls=%async_computation.2 | async-start | bytes 393216 | tf_op jit(solution)/shard_map/all_to_all | solution.py:176
  48.5 5.1 %collective-permute-start.3 = (bf16[1024,128]{1,0:T(8,128)(2,1)S(1)}, bf16[1024,128]{1,0:T(8,128)(2,1)S(1)}, u32[]{:S(2)}, u32[]{:S(2)}) collective-permute-start(bf16[1024,128]{1,0:T(8,128)(2,1)S(1)} %collective-permute-done.2.side_ref), channel_id=1, source_target_pairs={{0,1},{1,0},{2,3},{3,2},{4,5},{5,4},{6,7},{7,6},{8,9},{9,8},{10,11... | collective-permute-start | bytes 786440 | tf_op jit(solution)/shard_map/ppermute | solution.py:179
  50.5 2.2 %copy-start = (bf16[512,4096]{1,0:T(8,128)(2,1)S(1)}, bf16[512,4096]{1,0:T(8,128)(2,1)}, u32[]{:S(2)}) copy-start(bf16[512,4096]{1,0:T(8,128)(2,1)} %rows_ref.1) | copy-start | bytes 12582916
